TPU v7x, 128 devices: a whole 4x4x4 slice. The times are simulated.
128 devices in a mesh: fsdp: 32 (over x, y, core), tensor: 4 (over z).
Axes of the slice: x: 4, y: 4, z: 4, core: 2. Of those that a mesh axis runs over, the one named last changes fastest.
Arguments:
- momentum: float32 [8192, 26624], P('fsdp', 'tensor'), may hold values from -150 to 150
- gradient: bfloat16 [8192, 26624], P('fsdp', 'tensor'), may hold values from -6 to 6
- right_prev: float32 [256, 26624], P('fsdp', 'tensor'), may hold values from -0.0390625 to 0.0390625
Outputs:
- new_momentum: float32 [8192, 26624], P('fsdp', 'tensor')
- right_next: float32 [256, 26624], P('fsdp', 'tensor')
- update: bfloat16 [8192, 26624], P('fsdp', 'tensor')
All inputs are finite; a program needn't handle non-finite values.
Results may differ from a plain program's by a relative error of at most 0.0017.
Values sent between devices are 32-bit elements; how exact they have to be, the bound alone decides.
A program may use at most 128 MiB of HBM per device.

v0:
```python
import jax
import jax.numpy as jnp
from jax import lax
from jax.sharding import PartitionSpec as P

M_ROWS = 8192
N_COLS = 26624
RANK = 256


def orthonormalize(projected, gram_total):
    cholesky_low = jnp.linalg.cholesky(gram_total)
    return jax.scipy.linalg.solve_triangular(cholesky_low, projected.T, lower=True).T


def on_device(momentum, gradient, right_prev):
    highest = lax.Precision.HIGHEST
    buffer = momentum + gradient.astype(jnp.float32)
    partial_proj = lax.dot_general(
        buffer,
        lax.all_gather(right_prev, "fsdp", axis=0, tiled=True),
        (((1,), (1,)), ((), ())),
        precision=highest,
        preferred_element_type=jnp.float32,
    )
    projected = lax.psum(partial_proj, "tensor")
    gram_part = jnp.dot(
        projected.T, projected, precision=highest, preferred_element_type=jnp.float32
    )
    gram_total = lax.psum(gram_part, "fsdp")
    orthonormal = orthonormalize(projected, gram_total)
    rank_dev = right_prev.shape[0]
    right_part = jnp.dot(
        orthonormal.T, buffer, precision=highest, preferred_element_type=jnp.float32
    )
    right_full = lax.psum(right_part, "fsdp")
    squares = lax.psum(jnp.sum(right_full * right_full, axis=1), "tensor")
    col_norm = jnp.sqrt(squares) + 1e-06
    right_unit = right_full / col_norm[:, None]
    right_next = lax.dynamic_slice_in_dim(
        right_unit, lax.axis_index("fsdp") * rank_dev, rank_dev, 0
    )
    new_momentum = buffer - 0.05 * jnp.dot(
        orthonormal, right_full, precision=highest, preferred_element_type=jnp.float32
    )
    unit_scale = (M_ROWS * N_COLS / RANK) ** 0.5
    update = (
        unit_scale
        * jnp.dot(orthonormal, right_unit, precision=highest, preferred_element_type=jnp.float32)
    ).astype(jnp.bfloat16)
    return (new_momentum, right_next, update)


def solution(mesh):
    in_specs = (P("fsdp", "tensor"), P("fsdp", "tensor"), P("fsdp", "tensor"))
    out_specs = (P("fsdp", "tensor"), P("fsdp", "tensor"), P("fsdp", "tensor"))
    return jax.shard_map(
        on_device, mesh=mesh, in_specs=in_specs, out_specs=out_specs, check_vma=False
    )
```

profile of v0, /device:TPU:1, one launch (start us, length us, event | category | flops | bytes accessed | tf_op | source)
XLA Modules:
  0.0 475.9 jit_solution(2633410781211095108)
XLA Ops:
  7.2 0.0 all-gather.2.cloned.1.call-start
  7.2 0.7 all-gather.2.cloned.1.call-update
  7.9 0.0 all-reduce.5.cloned.1.call-start
  7.9 55.8 %all-gather.2.cloned.1.call-done = f32[256,6656]{1,0:T(8,128)} async-done(((f32[8,6656]{1,0:T(8,128)}), f32[256,6656]{1,0:T(8,128)}) %all-gather.2.cloned.1.call-update) | async-done | bytes 6815760 | tf_op jit(solution)/shard_map/all_gather | solution.py:21
  63.8 18.6 %fusion.3 = f32[256,256]{1,0:T(8,128)} fusion(f32[256,6656]{1,0:T(8,128)} %all-gather.2.cloned.1.call-done, f32[256,6656]{1,0:T(8,128)} %param.3, bf16[256,6656]{1,0:T(8,128)(2,1)} %param.4), kind=kOutput, calls=%fused_computation.10 | convolution fusion | flops 5237899264 | bytes 17301504 | tf_op jit(solution)/shard_map/dot_general | solution.py:19
  82.4 0.0 all-reduce.5.cloned.1.call-update
  82.5 0.0 all-reduce.7.cloned.1.call-start
  82.5 38.4 %all-reduce.5.cloned.1.call-done = f32[256,256]{1,0:T(8,128)} async-done(((f32[256,256]{1,0:T(8,128)}), f32[256,256]{1,0:T(8,128)}) %all-reduce.5.cloned.1.call-update) | async-done | bytes 262160 | tf_op jit(solution)/shard_map/psum | solution.py:26
  120.9 2.3 fusion.16
  123.3 0.0 all-reduce.7.cloned.1.call-update
  123.3 0.2 all-reduce.9.cloned.1.call-start
  123.5 105.0 %all-reduce.7.cloned.1.call-done = f32[256,256]{0,1:T(8,128)} async-done(((f32[256,256]{0,1:T(8,128)}), f32[256,256]{0,1:T(8,128)}) %all-reduce.7.cloned.1.call-update) | async-done | bytes 262160 | tf_op jit(solution)/shard_map/psum | solution.py:30
  228.6 1.8 copy.7
  230.3 1.1 fusion.4
  231.4 0.0 copy-start.5
  231.4 0.7 copy-done.5
  232.1 11.7 %cholesky.50 = f32[128,128]{1,0:T(8,128)S(1)} custom-call(f32[128,128]{1,0:T(8,128)S(1)} %cholesky.118), custom_call_target="Cholesky" | custom-call | tf_op jit(solution)/shard_map/jit(cholesky)/cholesky | solution.py:12
  243.9 10.4 %custom-call.15 = f32[1,128,128]{1,2,0:T(8,128)} custom-call(f32[1,128,128]{2,1,0:T(8,128)S(1)} %get-tuple-element.24), custom_call_target="InvertDiagBlocksLowerTriangular" | custom-call | tf_op jit(solution)/shard_map/jit(cholesky)/cholesky | solution.py:12
  254.3 0.7 cholesky.113
  255.0 1.7 constant_dynamic-update-slice_fusion
  256.7 1.1 convolution_subtract_fusion.1
  257.8 11.7 %cholesky.105 = f32[128,128]{1,0:T(8,128)S(1)} custom-call(f32[128,128]{1,0:T(8,128)S(1)} %convolution_subtract_fusion.1), custom_call_target="Cholesky" | custom-call | tf_op jit(solution)/shard_map/jit(cholesky)/cholesky | solution.py:12
  269.6 0.6 select_reduce_fusion
  270.2 0.6 compare_reduce_fusion
  272.0 1.7 select_select_fusion
  273.7 0.1 triangular_solve.57
  273.8 6.8 %while.1 = (s32[]{:T(128)}, f32[256,256]{1,0:T(8,128)}, s32[2,2]{1,0:T(2,128)S(1)}, f32[2,128,128]{2,1,0:T(8,128)}, s32[]{:T(128)}) while((s32[]{:T(128)}, f32[256,256]{1,0:T(8,128)}, s32[2,2]{1,0:T(2,128)S(1)}, f32[2,128,128]{2,1,0:T(8,128)}, s32[]{:T(128)}) %tuple.27), condition=%wide.while_cond, body=%wide.while_body.sunk | while | flops 2 | bytes 132705 | solution.py:13
  273.8 0.6 fusion.27
  274.4 2.8 bitcast_dynamic-update-slice_fusion.2
  277.2 0.6 fusion.27
  277.8 2.8 bitcast_dynamic-update-slice_fusion.2
  280.6 21.1 %custom-call.16 = f32[2,128,128]{1,2,0:T(8,128)} custom-call(f32[2,128,128]{2,1,0:T(8,128)} %get-tuple-element.10), custom_call_target="InvertDiagBlocksLowerTriangular" | custom-call | tf_op jit(solution)/shard_map/jit(_solve_triangular)/triangular_solve | solution.py:13
  301.7 1.3 fusion.5
  302.9 1.3 convolution_subtract_fusion
  304.3 1.2 fusion.8
  305.4 0.0 copy-start.3
  305.4 0.6 copy-done.3
  306.1 13.2 %fusion.2 = f32[256,6656]{1,0:T(8,128)} fusion(f32[256,6656]{1,0:T(8,128)} %param.3, bf16[256,6656]{1,0:T(8,128)(2,1)S(1)} %copy-done.1, f32[128,256]{1,0:T(8,128)S(1)} %fusion.8, f32[128,256]{1,0:T(8,128)S(1)} %fusion.5), kind=kOutput, calls=%fused_computation.9 | convolution fusion | flops 5237964800 | bytes 17301504 | tf_op jit(solution)/shard_map/dot_general | solution.py:33
  319.3 0.0 all-reduce.9.cloned.1.call-update
  319.3 116.5 %all-reduce.9.cloned.1.call-done = f32[256,6656]{1,0:T(8,128)} async-done(((f32[256,6656]{1,0:T(8,128)}), f32[256,6656]{1,0:T(8,128)}) %all-reduce.9.cloned.1.call-update) | async-done | bytes 6815760 | tf_op jit(solution)/shard_map/psum | solution.py:36
  435.8 3.6 multiply_reduce_fusion
  439.4 8.7 %psum.31 = f32[256]{0:T(256)S(1)} all-reduce(f32[256]{0:T(256)S(1)} %multiply_reduce_fusion), channel_id=1, replica_groups=mesh['fsdp'=32,'tensor'=4] {'tensor'}, use_global_device_ids=true, to_apply=%region_8.9 | all-reduce | flops 256 | bytes 2048 | tf_op jit(solution)/shard_map/psum | solution.py:37
  448.1 0.0 slice-start.1
  448.1 3.9 broadcast_divide_fusion
  452.0 0.0 copy-start.2
  452.0 7.5 %fusion.1 = bf16[256,6656]{1,0:T(8,128)(2,1)} fusion(f32[256,6656]{1,0:T(8,128)S(1)} %broadcast_divide_fusion, f32[128,256]{1,0:T(8,128)S(1)} %copy-done.4, f32[128,256]{1,0:T(8,128)S(1)} %fusion.5), kind=kOutput, calls=%fused_computation.5 | convolution fusion | flops 5237964800 | bytes 10485760 | tf_op jit(solution)/shard_map/dot_general | solution.py:49
  459.6 0.7 constant_dynamic-slice_fusion.1
  460.3 9.1 %fusion = f32[256,6656]{1,0:T(8,128)} fusion(f32[256,6656]{1,0:T(8,128)S(1)} %copy-done, f32[256,6656]{1,0:T(8,128)S(1)} %bitcast.38, bf16[256,6656]{1,0:T(8,128)(2,1)S(1)} %copy-done.2, f32[128,256]{1,0:T(8,128)S(1)} %copy-done.4, f32[128,256]{1,0:T(8,128)S(1)} %fusion.5), kind=kOutput, calls=%fused_computation.4 | convolution fusion | flops 5241372672 | bytes 24117248 | tf_op jit(solution)/shard_map/dot_general | solution.py:43
  (18 shorter events, 0.1 us)
Async XLA Ops:
  7.2 56.6 %all-gather.2.cloned.1.call-start = ((), (), s32[]{:S(2)}) async-start(), calls=%async_computation | async-start | bytes 7028736 | tf_op jit(solution)/shard_map/all_gather | solution.py:21
  7.9 113.0 %all-reduce.5.cloned.1.call-start = ((), (), s32[]{:S(2)}) async-start(), calls=%async_computation.1 | async-start | bytes 524288 | tf_op jit(solution)/shard_map/psum | solution.py:26
  82.4 223.7 %copy-start.1 = (bf16[256,6656]{1,0:T(8,128)(2,1)S(1)}, bf16[256,6656]{1,0:T(8,128)(2,1)}, u32[]{:S(2)}) copy-start(bf16[256,6656]{1,0:T(8,128)(2,1)} %param.4) | copy-start | bytes 10223620
  82.5 146.1 %all-reduce.7.cloned.1.call-start = ((), (), s32[]{:S(2)}) async-start(), calls=%async_computation.2 | async-start | bytes 524288 | tf_op jit(solution)/shard_map/psum | solution.py:30
  123.3 312.5 %all-reduce.9.cloned.1.call-start = ((), (), s32[]{:S(2)}) async-start(), calls=%async_computation.3 | async-start | bytes 13631488 | tf_op jit(solution)/shard_map/psum | solution.py:36
  231.4 0.7 copy-start.5
  305.4 0.7 copy-start.3
  435.8 24.5 %slice-start = ((s8[6815744]{0:T(1024)(128)(4,1)}), s8[2621440]{0:T(1024)(128)(4,1)S(1)}, s32[]{:S(2)}) async-start(s8[6815744]{0:T(1024)(128)(4,1)} %bitcast.37), calls=%async_computation.4 | async-start | bytes 5242880
  448.1 3.9 copy-start.4
  448.1 12.2 %slice-start.1 = ((s8[6815744]{0:T(1024)(128)(4,1)}), s8[4194304]{0:T(1024)(128)(4,1)S(1)}, s32[]{:S(2)}) async-start(s8[6815744]{0:T(1024)(128)(4,1)} %bitcast.37), calls=%async_computation.5 | async-start | bytes 8388608
  452.0 8.2 %copy-start = (f32[256,6656]{1,0:T(8,128)S(1)}, f32[256,6656]{1,0:T(8,128)}, u32[]{:S(2)}) copy-start(f32[256,6656]{1,0:T(8,128)} %all-reduce.9.cloned.1.call-done) | copy-start | bytes 20447236
  452.0 8.2 %copy-start.2 = (bf16[256,6656]{1,0:T(8,128)(2,1)S(1)}, bf16[256,6656]{1,0:T(8,128)(2,1)}, u32[]{:S(2)}) copy-start(bf16[256,6656]{1,0:T(8,128)(2,1)} %param.4) | copy-start | bytes 10223620
Sparse Core Ops, SparseCore 0:
  10.2 53.4 all-gather.1
  82.6 38.3 all-reduce.4
  125.1 103.4 all-reduce.6
  319.4 116.3 all-reduce.8
where the time goes:
time: 478 us; the launch traced here: 476 us
  waiting for transfers between devices  316 us (66%)
  other arithmetic  66.6 us (14%)
  matrix products  57.3 us (12%)
  between operations  15.1 us (3%)
  local copies, waits for them, and re-layouts  11.4 us (2%)
  blocking collectives  8.66 us (2%)
    psum x1, waiting for transfers between devices, on_device(): right_full = lax.psum(right_part, 'fsdp')  116 us
    psum x1, waiting for transfers between devices, on_device(): gram_total = lax.psum(gram_part, 'fsdp')  105 us
    all_gather x1, waiting for transfers between devices, on_device(): lax.all_gather(right_prev, 'fsdp', axis=0, tiled=True)  55.8 us
    psum x1, waiting for transfers between devices, on_device(): projected = lax.psum(partial_proj, 'tensor')  38.4 us
    another operation x6, other arithmetic, orthonormalize(): cholesky_low = jnp.linalg.cholesky(gram_total)  35.2 us
    another operation x3, other arithmetic, orthonormalize(): jax.scipy.linalg.solve_triangular(cholesky_low, projected.T, lower=True)  22.8 us
    dot_general x1, matrix products, on_device(): lax.dot_general(buffer, lax.all_gather(right_prev, 'fsdp', axis=0, tiled=...  18.6 us
    dot_general x1, matrix products, on_device(): jnp.dot(orthonormal.T, buffer, precision=highest, preferred_element_type=...  13.2 us
  transfers between devices with their start and end apart: 4, of which 4 were waited for; matrix products, arithmetic and copies ran while one was open for 0% of the time, Pallas kernels for 0%

commit v1 on v0

v1 whole, which is shorter than its diff:
```python
import jax
import jax.numpy as jnp
from jax import lax
from jax.experimental import pallas as pl
from jax.experimental.pallas import tpu as pltpu
from jax.sharding import PartitionSpec as P

M_ROWS = 8192
N_COLS = 26624
RANK = 256
F32 = jnp.float32
BF16 = jnp.bfloat16
MESH = pl.DeviceIdType.MESH
HIGHEST = lax.Precision.HIGHEST

ROWS = 256
COLS = 6656
HALF = COLS // 2
STREAM = HALF // 2
PIECE = STREAM // 16
CUT = 56
CHUNK = 256
N_CHUNK = HALF // CHUNK
N_SEM = 176


def split(a):
    high = a.astype(BF16)
    return high, (a - high.astype(F32)).astype(BF16)


def dot(a, b, precision=None):
    return jnp.dot(a, b, precision=precision, preferred_element_type=F32)


def dot_nt(a, b, precision=None):
    return lax.dot_general(
        a, b, (((1,), (1,)), ((), ())), precision=precision, preferred_element_type=F32
    )


def dot_tn(a, b, precision=None):
    return lax.dot_general(
        a, b, (((0,), (0,)), ((), ())), precision=precision, preferred_element_type=F32
    )


def row_of(v, i):
    return jnp.broadcast_to(v[i : i + 1, :], v.shape)


def factor_panel(work, base, panel):
    first = base + 8 * panel
    sub = lax.broadcasted_iota(jnp.int32, (8, 128), 0)
    lane = lax.broadcasted_iota(jnp.int32, (8, 128), 1)
    rows = pl.ds(pl.multiple_of(first, 8), 8)
    parts = [work[rows, 128 * t : 128 * t + 128] for t in range(4)]
    here = pltpu.roll(parts[base // 128], lax.rem(128 - 8 * panel, 128), 1)
    cols = [jnp.broadcast_to(here[:, i : i + 1], (8, 128)) for i in range(8)]
    for i in range(8):
        inv = lax.rsqrt(row_of(cols[i], i))
        coef = jnp.where(sub > i, cols[i] * inv, 0.0)
        for t in range(4):
            scaled = row_of(parts[t], i) * inv
            parts[t] = jnp.where(sub == i, scaled, parts[t] - coef * scaled)
        for j in range(i + 1, 8):
            cols[j] = cols[j] - coef * (row_of(cols[j], i) * inv)
    for t in range(4):
        work[rows, 128 * t : 128 * t + 128] = parts[t]
    left = jnp.where(lane > 8 * panel + 7, parts[base // 128], 0.0)
    whole = jnp.concatenate(parts, axis=1)
    work[base : base + 128, :] = work[base : base + 128, :] - dot_tn(left, whole, HIGHEST)


def kernel(
    m_hbm, g_hbm, v_in, wt_out, lhs_out, m8_out,
    m_v, g_v, bts, btr, bh, bl, vb, pt, ptr, zr, pts, ph, plo,
    gx, gy, gg, wt, r1p, r1m, r2, r3, wown, work, sx, sy, sz, sc, q_s,
    ss, rs, ls,
):
    f = lax.axis_index("fsdp")
    z = lax.axis_index("tensor")
    x, y, c = f // 8, lax.rem(f // 2, 4), lax.rem(f, 2)
    q_me = 4 * x + y

    def mod(i):
        return lax.rem(i + 8, 4)

    def dev(xx, yy, cc, zz):
        return (mod(xx) * 8 + mod(yy) * 2 + cc, mod(zz))

    sib = dev(x, y, 1 - c, z)
    n_used = [0]

    def take(n):
        at = n_used[0]
        n_used[0] += n
        assert n_used[0] <= N_SEM
        return at

    def send(src, dst, to, i):
        return pltpu.make_async_remote_copy(
            src_ref=src, dst_ref=dst, send_sem=ss.at[i], recv_sem=rs.at[i],
            device_id=to, device_id_type=MESH,
        )

    pending = []

    def start(src, dst, to, i):
        copy = send(src, dst, to, i)
        copy.start()
        pending.append(copy)

    def arrived(dst, i):
        send(dst, dst, sib, i).wait_recv()

    def sent():
        for copy in pending:
            copy.wait_send()
        pending.clear()

    bar = pltpu.get_barrier_semaphore()
    peers = [sib]
    for d in (1, 2, 3):
        peers += [dev(x + d, y, c, z), dev(x, y + d, c, z), dev(x, y, c, z + d)]
    for peer in peers:
        pl.semaphore_signal(bar, inc=1, device_id=peer, device_id_type=MESH)
    loads = []
    for h in range(2):
        half = (1 - c) if h == 0 else c
        at = pl.ds(pl.multiple_of(half * HALF, 128), HALF)
        loads.append(pltpu.make_async_copy(m_hbm.at[:, at], m_v.at[h], ls.at[2 * h]))
        loads.append(pltpu.make_async_copy(g_hbm.at[:, at], g_v.at[h], ls.at[2 * h + 1]))
    for load in loads:
        load.start()
    pl.semaphore_wait(bar, len(peers))

    def ab(s):
        return (x, y) if s == 0 else (y, x)

    def dev_ab(s, a, b):
        return dev(a, b, c, z) if s == 0 else dev(b, a, c, z)

    class Gather:
        def __init__(self, piece, half, own, after=None):
            self.piece, self.half, self.own = piece, half, own
            self.small = [take(3), take(3)]
            self.big = [take(8), take(8)]
            self.forward = [take(8), take(8)]

        def spread(self, s, k, src):
            a, b = ab(s)
            here = self.piece(s, a, mod(b + k))
            start(src, here, dev_ab(s, a + 1, b), self.big[s] + k)
            start(src, here, dev_ab(s, a - 1, b), self.big[s] + 4 + k)

        def begin(self):
            for s in range(2):
                a, b = ab(s)
                for d in (1, 3, 2):
                    start(self.own(s), self.piece(s, a, b), dev_ab(s, a, b + d), self.small[s] + d - 1)
                self.spread(s, 0, self.own(s))

        def middle(self, d):
            for s in range(2):
                a, b = ab(s)
                piece = self.piece(s, a, mod(b - d))
                arrived(piece, self.small[s] + d - 1)
                self.spread(s, 4 - d, piece)

        def relay(self, k):
            for s in range(2):
                a, b = ab(s)
                bb = mod(b + k)
                arrived(self.piece(s, mod(a - 1), bb), self.big[s] + k)
                plus = self.half(s, mod(a - 1), bb, 0)
                start(plus, plus, dev_ab(s, a + 1, b), self.forward[s] + k)
                arrived(self.piece(s, mod(a + 1), bb), self.big[s] + 4 + k)
                minus = self.half(s, mod(a + 1), bb, 1)
                start(minus, minus, dev_ab(s, a - 1, b), self.forward[s] + 4 + k)

        def finish(self, k):
            for s in range(2):
                a, b = ab(s)
                bb = mod(b + k)
                arrived(self.half(s, mod(a + 2), bb, 0), self.forward[s] + k)
                arrived(self.half(s, mod(a + 2), bb, 1), self.forward[s] + 4 + k)

    i_v = take(2)
    for s in range(2):
        theirs = pl.ds(pl.multiple_of((1 - c) * HALF + s * STREAM, 128), STREAM)
        start(v_in.at[:, theirs], vb.at[s, q_me, pl.ds(8 * c, 8)], sib, i_v + s)
    for s in range(2):
        mine = pl.ds(pl.multiple_of(c * HALF + s * STREAM, 128), STREAM)
        vb[s, q_me, pl.ds(pl.multiple_of(8 * c, 8), 8), :] = v_in[:, mine]
    for s in range(2):
        arrived(vb.at[s, q_me, pl.ds(8 * (1 - c), 8)], i_v + s)

    def v_piece(s, a, b):
        return vb.at[s, 4 * a + b] if s == 0 else vb.at[s, 4 * b + a]

    def v_half(s, a, b, h):
        return v_piece(s, a, b).at[pl.ds(8 * h, 8)]

    gather_v = Gather(v_piece, v_half, lambda s: v_piece(s, *ab(s)))
    gather_v.begin()

    i_b = take(N_CHUNK)
    loads[0].wait()
    loads[1].wait()

    def b_send(j):
        return send(bts.at[j], btr.at[j], sib, i_b + j)

    def other_chunk(j, carry):
        at = pl.ds(pl.multiple_of(j * CHUNK, CHUNK), CHUNK)
        bts[j] = (m_v[0, :, at] + g_v[0, :, at].astype(F32)).T
        b_send(j).start()
        return carry

    def own_chunk(j, carry):
        at = pl.ds(pl.multiple_of(j * CHUNK, CHUNK), CHUNK)
        high, low = split((m_v[1, :, at] + g_v[1, :, at].astype(F32)).T)
        bh[at, 0:ROWS] = high
        bl[at, 0:ROWS] = low
        return carry

    def sibling_chunk(j, carry):
        b_send(j).wait()
        at = pl.ds(pl.multiple_of(j * CHUNK, CHUNK), CHUNK)
        high, low = split(btr[j])
        bh[at, ROWS:] = high
        bl[at, ROWS:] = low
        return carry

    lax.fori_loop(0, N_CHUNK, other_chunk, 0)
    gather_v.middle(1)
    gather_v.middle(3)
    gather_v.middle(2)
    loads[2].wait()
    loads[3].wait()
    lax.fori_loop(0, N_CHUNK, own_chunk, 0)
    gather_v.relay(0)
    lax.fori_loop(0, N_CHUNK, sibling_chunk, 0)
    for k in (3, 1, 2):
        gather_v.relay(k)
    for k in (0, 3, 1, 2):
        gather_v.finish(k)

    for s in range(2):
        span = slice(s * STREAM, (s + 1) * STREAM)

        def project(g, carry):
            rows = vb[s, pl.ds(4 * g, 4)].reshape(64, STREAM)
            high, low = split(rows)
            part = dot(high, bh[span, :]) + dot(high, bl[span, :]) + dot(low, bh[span, :])
            at = pl.ds(pl.multiple_of(64 * g, 64), 64)
            if s == 0:
                pt[at, :] = part
            else:
                pt[at, :] = pt[at, :] + part
            return carry

        lax.fori_loop(0, 4, project, 0)
    sent()
    i_p = take(1)
    start(pt.at[:, ROWS:], ptr, sib, i_p)
    arrived(ptr, i_p)
    zr[0] = pt[:, 0:ROWS] + ptr[...]
    near = z + 1 - 2 * lax.rem(z, 2)
    far = 3 - z
    i_z = take(4)
    tops = (pl.ds(0, 128), pl.ds(128, 128))
    for step in range(2):
        for h in range(2):
            to = near if h == step else far
            start(zr.at[2 * step, tops[h]], zr.at[2 * step + 1, tops[h]], dev(x, y, c, to), i_z + 2 * step + h)
        for h in range(2):
            arrived(zr.at[2 * step + 1, tops[h]], i_z + 2 * step + h)
            zr[2 * step + 2, tops[h], :] = zr[2 * step, tops[h], :] + zr[2 * step + 1, tops[h], :]
    p_own = zr.at[4]
    i_s = take(1)
    start(p_own, pts, sib, i_s)
    high, low = split(p_own[...].T)
    ph[0:ROWS, :] = high
    plo[0:ROWS, :] = low
    arrived(pts, i_s)
    high, low = split(pts[...].T)
    ph[ROWS:, :] = high
    plo[ROWS:, :] = low

    def exchange(slots, at, where, i):
        for d in (1, 2, 3):
            start(slots.at[at], slots.at[at], where(at + d), i + d - 1)

    def exchanged(slots, at, i):
        for d in (1, 2, 3):
            arrived(slots.at[mod(at - d)], i + d - 1)
        return slots[0] + slots[1] + slots[2] + slots[3]

    share = pl.ds(pl.multiple_of(32 * (2 * z + c), 32), 32)
    gx[x] = dot_nt(zr[4, share, :], p_own[...], HIGHEST) + dot_nt(pts[share, :], pts[...], HIGHEST)
    i_gx, i_gy, i_gz, i_gc = take(3), take(3), take(3), take(1)
    exchange(gx, x, lambda to: dev(to, y, c, z), i_gx)

    def right_part(s, a):
        row = pl.multiple_of(s * STREAM + a * 4 * PIECE, 16)
        at = pl.ds(row, 4 * PIECE)
        part = dot(bh[at, :], ph[...]) + dot(bh[at, :], plo[...]) + dot(bl[at, :], ph[...])
        wt[pl.ds(16 * s + 4 * a, 4)] = part.reshape(4, PIECE, RANK)

    i_r1, i_r2, i_r3 = take(4), take(4), take(6)
    low_cut, high_cut = pl.ds(0, CUT), pl.ds(CUT, PIECE - CUT)

    def group(s, a):
        return pl.ds(16 * s + 4 * mod(a), 4)

    for s in range(2):
        a, b = ab(s)
        right_part(s, mod(a + 2))
        start(wt.at[group(s, a + 2), low_cut], r1p.at[s], dev_ab(s, a + 1, b), i_r1 + 2 * s)
        start(wt.at[group(s, a + 2), high_cut], r1m.at[s], dev_ab(s, a - 1, b), i_r1 + 2 * s + 1)
    for s in range(2):
        a, b = ab(s)
        right_part(s, mod(a + 1))
        right_part(s, mod(a - 1))
    gy[y] = exchanged(gx, x, i_gx)
    exchange(gy, y, lambda to: dev(x, to, c, z), i_gy)
    for s in range(2):
        a, b = ab(s)
        right_part(s, a)
    for s in range(2):
        a, b = ab(s)
        up, down = group(s, a + 1), group(s, a - 1)
        arrived(r1p.at[s], i_r1 + 2 * s)
        wt[up, 0:CUT, :] = wt[up, 0:CUT, :] + r1p[s]
        start(wt.at[up], r2.at[s, 0], dev_ab(s, a + 1, b), i_r2 + 2 * s)
        arrived(r1m.at[s], i_r1 + 2 * s + 1)
        wt[down, CUT:, :] = wt[down, CUT:, :] + r1m[s]
        start(wt.at[down], r2.at[s, 1], dev_ab(s, a - 1, b), i_r2 + 2 * s + 1)
    gg[z, c] = exchanged(gy, y, i_gy)
    for d in (1, 2, 3):
        start(gg.at[z, c], gg.at[z, c], dev(x, y, c, z + d), i_gz + d - 1)
    for d in (1, 2, 3):
        arrived(gg.at[mod(z - d), c], i_gz + d - 1)
    start(gg.at[:, c], gg.at[:, c], sib, i_gc)
    arrived(gg.at[:, 1 - c], i_gc)
    work[:, 0:RANK] = gg[...].reshape(RANK, RANK)
    eye = lax.broadcasted_iota(jnp.int32, (RANK, RANK), 0) == lax.broadcasted_iota(
        jnp.int32, (RANK, RANK), 1
    )
    work[:, RANK:] = eye.astype(F32)

    def panels(base, low, high):
        def one(p, carry):
            factor_panel(work, base, p)
            return carry

        lax.fori_loop(low, high, one, 0)

    panels(0, 0, 8)

    def own_idx(s):
        a, b = ab(s)
        return 16 * s + 4 * a + b

    for s in range(2):
        a, b = ab(s)
        here = group(s, a)
        for k in range(2):
            arrived(r2.at[s, k], i_r2 + 2 * s + k)
        wt[here] = wt[here] + r2[s, 0] + r2[s, 1]
        for d in (1, 3, 2):
            start(wt.at[16 * s + 4 * a + mod(b + d)], r3.at[s, d - 1], dev_ab(s, a, b + d), i_r3 + 3 * s + d - 1)
    panels(0, 8, 12)
    keeps = []
    for s in range(2):
        for d in (1, 3, 2):
            arrived(r3.at[s, d - 1], i_r3 + 3 * s + d - 1)
        wown[s] = wt[own_idx(s)] + r3[s, 0] + r3[s, 1] + r3[s, 2]
        keep = pltpu.make_async_copy(wown.at[s], wt_out.at[32 * c + own_idx(s)], ls.at[4 + s])
        keep.start()
        keeps.append(keep)

    def w_piece(s, a, b):
        return wt_out.at[32 * c + 16 * s + 4 * a + b]

    def w_half(s, a, b, h):
        return w_piece(s, a, b).at[low_cut if h == 0 else high_cut]

    i_w = take(8)

    def hand_over(n, a_of):
        for s in range(2):
            a = a_of(ab(s)[0])
            at = wt_out.at[pl.ds(32 * c + 16 * s + 4 * a, 4)]
            start(at, at, sib, i_w + 2 * n + s)

    gather_w = Gather(w_piece, w_half, lambda s: wown.at[s])
    gather_w.begin()
    panels(0, 12, 16)
    work[128:, :] = work[128:, :] - dot_tn(work[0:128, 128:256], work[0:128, :], HIGHEST)
    gather_w.middle(1)
    gather_w.middle(3)
    gather_w.middle(2)
    for keep in keeps:
        keep.wait()
    hand_over(0, lambda a: a)
    panels(128, 0, 6)
    gather_w.relay(0)
    panels(128, 6, 12)
    gather_w.relay(3)
    panels(128, 12, 16)
    gather_w.relay(1)

    low_inv = work.at[:, pl.ds(RANK, RANK)]
    total = jnp.zeros((1, RANK), F32)
    for s in range(2):
        right = dot_nt(wown[s], low_inv[...], HIGHEST)
        total = total + jnp.sum(right * right, axis=0, keepdims=True)
    i_qx, i_qy, i_qz, i_qc = take(3), take(3), take(3), take(1)
    sx[x] = jnp.broadcast_to(total, (8, RANK))
    exchange(sx, x, lambda to: dev(to, y, c, z), i_qx)
    gather_w.relay(2)
    hand_over(1, lambda a: mod(a - 1))
    hand_over(2, lambda a: mod(a + 1))
    q_s[...] = dot_nt(jnp.transpose(p_own[...]), low_inv[...], HIGHEST)
    lhs_out[ROWS:, :] = -0.05 * dot(q_s[...], low_inv[...], HIGHEST)
    sy[y] = exchanged(sx, x, i_qx)
    exchange(sy, y, lambda to: dev(x, to, c, z), i_qy)
    sz[z] = exchanged(sy, y, i_qy)
    exchange(sz, z, lambda to: dev(x, y, c, to), i_qz)
    sc[c] = exchanged(sz, z, i_qz)
    start(sc.at[c], sc.at[c], sib, i_qc)
    arrived(sc.at[1 - c], i_qc)
    norm = 1.0 / (jnp.sqrt((sc[0] + sc[1])[0:1, :]) + 1e-06)
    unit_scale = (M_ROWS * N_COLS / RANK) ** 0.5
    lhs_out[0:ROWS, :] = dot(q_s[...] * (unit_scale * norm), low_inv[...], HIGHEST)
    pick = lax.broadcasted_iota(jnp.int32, (16, RANK), 1) == (
        8 * f + lax.broadcasted_iota(jnp.int32, (16, RANK), 0)
    )
    m8_out[...] = dot(jnp.where(pick, norm, 0.0), low_inv[...], HIGHEST)
    for k in (0, 3, 1, 2):
        gather_w.finish(k)
    hand_over(3, lambda a: mod(a + 2))
    for n, step in enumerate((0, -1, 1, 2)):
        for s in range(2):
            a = mod(ab(s)[0] + step)
            arrived(wt_out.at[pl.ds(32 * (1 - c) + 16 * s + 4 * a, 4)], i_w + 2 * n + s)
    sent()


def reduce_right(momentum, gradient, right_prev):
    vmem = pltpu.VMEM
    any_space = pl.BlockSpec(memory_space=pl.ANY)
    in_vmem = pl.BlockSpec(memory_space=pltpu.VMEM)
    return pl.pallas_call(
        kernel,
        out_shape=(
            jax.ShapeDtypeStruct((64, PIECE, RANK), F32),
            jax.ShapeDtypeStruct((2 * ROWS, RANK), F32),
            jax.ShapeDtypeStruct((16, RANK), F32),
        ),
        in_specs=[any_space, any_space, in_vmem],
        out_specs=(any_space, in_vmem, in_vmem),
        scratch_shapes=[
            vmem((2, ROWS, HALF), F32),
            vmem((2, ROWS, HALF), BF16),
            vmem((N_CHUNK, CHUNK, ROWS), F32),
            vmem((N_CHUNK, CHUNK, ROWS), F32),
            vmem((HALF, 2 * ROWS), BF16),
            vmem((HALF, 2 * ROWS), BF16),
            vmem((2, 16, 16, STREAM), F32),
            vmem((RANK, 2 * ROWS), F32),
            vmem((RANK, ROWS), F32),
            vmem((5, RANK, ROWS), F32),
            vmem((RANK, ROWS), F32),
            vmem((2 * ROWS, RANK), BF16),
            vmem((2 * ROWS, RANK), BF16),
            vmem((4, 32, RANK), F32),
            vmem((4, 32, RANK), F32),
            vmem((4, 2, 32, RANK), F32),
            vmem((32, PIECE, RANK), F32),
            vmem((2, 4, CUT, RANK), F32),
            vmem((2, 4, PIECE - CUT, RANK), F32),
            vmem((2, 2, 4, PIECE, RANK), F32),
            vmem((2, 3, PIECE, RANK), F32),
            vmem((2, PIECE, RANK), F32),
            vmem((RANK, 2 * RANK), F32),
            vmem((4, 8, RANK), F32),
            vmem((4, 8, RANK), F32),
            vmem((4, 8, RANK), F32),
            vmem((2, 8, RANK), F32),
            vmem((ROWS, RANK), F32),
            pltpu.SemaphoreType.DMA((N_SEM,)),
            pltpu.SemaphoreType.DMA((N_SEM,)),
            pltpu.SemaphoreType.DMA((6,)),
        ],
        compiler_params=pltpu.CompilerParams(
            collective_id=0, has_side_effects=True, vmem_limit_bytes=56 * 2**20
        ),
        name="reduce_right",
    )(momentum, gradient, right_prev)


def finish_kernel(m_ref, g_ref, wt_ref, lhs_ref, m8_ref, new_ref, right_ref, update_ref):
    high, low = split(wt_ref[...])
    lhs_high, lhs_low = split(lhs_ref[0:ROWS, :])
    feed = lhs_ref[ROWS:, :].astype(BF16)
    new_ref[...] = m_ref[...] + g_ref[...].astype(F32) + dot_nt(feed, high)
    update = dot_nt(lhs_high, high) + dot_nt(lhs_high, low) + dot_nt(lhs_low, high)
    update_ref[...] = update.astype(BF16)
    m8_high, m8_low = split(m8_ref[...])
    right = dot_nt(m8_high, high) + dot_nt(m8_high, low) + dot_nt(m8_low, high)
    right_ref[...] = right[0:8, :]


def finish(momentum, gradient, wt, lhs, m8):
    wide = 512
    return pl.pallas_call(
        finish_kernel,
        grid=(COLS // wide,),
        out_shape=(
            jax.ShapeDtypeStruct((ROWS, COLS), F32),
            jax.ShapeDtypeStruct((8, COLS), F32),
            jax.ShapeDtypeStruct((ROWS, COLS), BF16),
        ),
        in_specs=[
            pl.BlockSpec((ROWS, wide), lambda j: (0, j)),
            pl.BlockSpec((ROWS, wide), lambda j: (0, j)),
            pl.BlockSpec((wide, RANK), lambda j: (j, 0)),
            pl.BlockSpec((2 * ROWS, RANK), lambda j: (0, 0)),
            pl.BlockSpec((16, RANK), lambda j: (0, 0)),
        ],
        out_specs=(
            pl.BlockSpec((ROWS, wide), lambda j: (0, j)),
            pl.BlockSpec((8, wide), lambda j: (0, j)),
            pl.BlockSpec((ROWS, wide), lambda j: (0, j)),
        ),
        compiler_params=pltpu.CompilerParams(vmem_limit_bytes=32 * 2**20),
        name="finish",
    )(momentum, gradient, wt, lhs, m8)


def on_device(momentum, gradient, right_prev):
    wt, lhs, m8 = reduce_right(momentum, gradient, right_prev)
    return finish(momentum, gradient, wt.reshape(COLS, RANK), lhs, m8)


def solution(mesh):
    spec = P("fsdp", "tensor")
    return jax.shard_map(
        on_device, mesh=mesh, in_specs=(spec,) * 3, out_specs=(spec,) * 3, check_vma=False
    )
```

time: 478 us -> 138 us (0.29)
  waiting for transfers between devices: 316 us -> 0 us
  Pallas kernels: 0 us -> 131 us
  other arithmetic: 66.6 us -> 0 us
  matrix products: 57.3 us -> 0 us
  between operations: 15.1 us -> 0.67 us
  blocking collectives: 8.66 us -> 0 us
    psum x3 -> x0, waiting for transfers between devices: 260 us -> none  [the longest x1 116 us: on_device(): right_full = lax.psum(right_part, 'fsdp')]
    pallas_call x0 -> x2, Pallas kernels: none -> 131 us  [the longest x1 121 us: reduce_right(): pl.pallas_call(kernel, out_shape=(jax.ShapeDtypeStruct((64, PIECE, RANK),...]
    another operation x9 -> x0, other arithmetic: 58 us -> none  [the longest x6 35.2 us: orthonormalize(): cholesky_low = jnp.linalg.cholesky(gram_total)]
    all_gather x1 -> x0, waiting for transfers between devices: 55.8 us -> none  [on_device(): lax.all_gather(right_prev, 'fsdp', axis=0, tiled=True)]
    dot_general x5 -> x0, matrix products: 50.8 us -> none  [the longest x1 18.6 us: on_device(): lax.dot_general(buffer, lax.all_gather(right_prev, 'fsdp', axis=0, tiled=...]
    psum x1 -> x0, blocking collectives: 8.66 us -> none  [on_device(): squares = lax.psum(jnp.sum(right_full * right_full, axis=1), 'tensor')]
    another operation x9 -> x0, local copies, waits for them, and re-layouts: 7.56 us -> none
    another operation x5 -> x0, matrix products: 6.55 us -> none  [the longest x3 3.74 us: orthonormalize(): jax.scipy.linalg.solve_triangular(cholesky_low, projected.T, lower=True)]
  transfers between devices with their start and end apart: 4 -> 0, of which waited for: 4 -> 0; matrix products, arithmetic and copies ran while one was open for 0% -> 0% of each run, Pallas kernels for 0% -> 0%
where the time goes in v1:
time: 138 us
  Pallas kernels  131 us (95%)
  local copies, waits for them, and re-layouts  6.65 us (5%)
    pallas_call x1, Pallas kernels, reduce_right(): pl.pallas_call(kernel, out_shape=(jax.ShapeDtypeStruct((64, PIECE, RANK),...  121 us
    pallas_call x1, Pallas kernels, finish(): pl.pallas_call(finish_kernel, grid=(COLS // wide,), out_shape=(jax.ShapeD...  9.67 us
    unnamed x10, local copies, waits for them, and re-layouts  6.65 us

profile of v1, /device:TPU:1, one launch (start us, length us, event | category | flops | bytes accessed | tf_op | source)
XLA Modules:
  0.0 138.1 jit_solution(10378662183243161749)
XLA Ops:
  0.6 0.0 copy-start
  0.6 121.1 %reduce_right.1 = (f32[64,104,256]{2,1,0:T(8,128)}, f32[512,256]{1,0:T(8,128)}, f32[16,256]{1,0:T(8,128)}) custom-call(f32[256,6656]{1,0:T(8,128)} %m_ref.1, bf16[256,6656]{1,0:T(8,128)(2,1)} %g_ref.1, f32[8,6656]{1,0:T(8,128)} %v_in.1), custom_call_target="tpu_custom_call" | custom-call | tf_op jit(solution)/shard_map/reduce_right/pallas_call | solution.py:457
  121.7 0.0 copy-done
  121.8 0.0 copy-start.1
  121.8 2.0 %copy-done.1 = bf16[256,6656]{1,0:T(8,128)(2,1)S(1)} copy-done((bf16[256,6656]{1,0:T(8,128)(2,1)S(1)}, bf16[256,6656]{1,0:T(8,128)(2,1)}, u32[]{:S(2)}) %copy-start.1) | copy-done | bytes 3407896
  123.7 0.0 copy-start.2
  123.7 2.9 %copy-done.2 = f32[64,104,256]{2,1,0:T(8,128)S(1)} copy-done((f32[64,104,256]{2,1,0:T(8,128)S(1)}, f32[64,104,256]{2,1,0:T(8,128)}, u32[]{:S(2)}) %copy-start.2) | copy-done | bytes 6815768
  126.7 0.0 copy-start.3
  126.7 1.0 copy-done.3
  127.7 0.0 copy-start.4
  127.7 0.7 copy-done.4
  128.4 9.7 %finish.1 = (f32[256,6656]{1,0:T(8,128)}, f32[8,6656]{1,0:T(8,128)}, bf16[256,6656]{1,0:T(8,128)(2,1)}) custom-call(f32[256,6656]{1,0:T(8,128)S(1)} %copy-done, bf16[256,6656]{1,0:T(8,128)(2,1)S(1)} %copy-done.1, f32[6656,256]{1,0:T(8,128)S(1)} %bitcast.1, f32[512,256]{1,0:T(8,128)S(1)} %copy-done.3, f32[16,256]{1,0:T(8,128)S(1)} %copy-done.4), custom_call_target="tpu_custom_call" | custom-call | tf_op jit(solution)/shard_map/finish/pallas_call | solution.py:520
Async XLA Ops:
  0.6 121.1 %copy-start = (f32[256,6656]{1,0:T(8,128)S(1)}, f32[256,6656]{1,0:T(8,128)}, u32[]{:S(2)}) copy-start(f32[256,6656]{1,0:T(8,128)} %m_ref.1) | copy-start | bytes 20447236
  121.8 2.0 %copy-start.1 = (bf16[256,6656]{1,0:T(8,128)(2,1)S(1)}, bf16[256,6656]{1,0:T(8,128)(2,1)}, u32[]{:S(2)}) copy-start(bf16[256,6656]{1,0:T(8,128)(2,1)} %g_ref.1) | copy-start | bytes 10223620
  123.7 2.9 %copy-start.2 = (f32[64,104,256]{2,1,0:T(8,128)S(1)}, f32[64,104,256]{2,1,0:T(8,128)}, u32[]{:S(2)}) copy-start(f32[64,104,256]{2,1,0:T(8,128)} %get-tuple-element.6) | copy-start | bytes 20447236
  126.7 1.0 copy-start.3
  127.7 0.7 copy-start.4

commit v2 on v1

v2 whole, which is shorter than its diff:
```python
import jax
import jax.numpy as jnp
from jax import lax
from jax.experimental import pallas as pl
from jax.experimental.pallas import tpu as pltpu
from jax.sharding import PartitionSpec as P

M_ROWS = 8192
N_COLS = 26624
RANK = 256
F32 = jnp.float32
BF16 = jnp.bfloat16
MESH = pl.DeviceIdType.MESH
HIGHEST = lax.Precision.HIGHEST

ROWS = 256
COLS = 6656
HALF = COLS // 2
STREAM = HALF // 2
PIECE = STREAM // 16
V_SUB = ((0, 896), (896, STREAM - 896))
W_SUB = ((0, 56), (56, 48))
W_HALF = (((0, 32), (32, 24)), ((56, 24), (80, 24)))
MAIN_MIB = 42
FINISH_MIB = 22
WIDE = 1664
BLOCK = 16
CHUNK = 256
N_CHUNK = HALF // CHUNK
N_SEM = 288

def split(a):
    high = a.astype(BF16)
    return high, (a - high.astype(F32)).astype(BF16)

def dot(a, b, precision=None):
    return jnp.dot(a, b, precision=precision, preferred_element_type=F32)

def dot_nt(a, b, precision=None):
    return lax.dot_general(
        a, b, (((1,), (1,)), ((), ())), precision=precision, preferred_element_type=F32
    )

def dot_tn(a, b, precision=None):
    return lax.dot_general(
        a, b, (((0,), (0,)), ((), ())), precision=precision, preferred_element_type=F32
    )

def row_of(v, i):
    return jnp.broadcast_to(v[i : i + 1, :], v.shape)

def thirds(a):
    one = a.astype(BF16).astype(F32)
    rest = a - one
    two = rest.astype(BF16).astype(F32)
    return one, two, rest - two

def outer(left, right):
    l1, l2, l3 = thirds(left)
    r1, r2, r3 = thirds(right)
    a = jnp.concatenate([l1, l1, l2, l1, l2, l3], axis=0).astype(BF16)
    b = jnp.concatenate([r1, r2, r1, r3, r2, r1], axis=0).astype(BF16)
    return dot_tn(a, b)

def factor_panel(work, base, panel):
    first = base + BLOCK * panel
    sub = lax.broadcasted_iota(jnp.int32, (BLOCK, 128), 0)
    lane = lax.broadcasted_iota(jnp.int32, (BLOCK, 128), 1)
    rows = pl.ds(pl.multiple_of(first, BLOCK), BLOCK)
    parts = [work[rows, 128 * t : 128 * t + 128] for t in range(4)]
    here = pltpu.roll(parts[base // 128], lax.rem(128 - BLOCK * panel, 128), 1)
    cols = [jnp.broadcast_to(here[:, i : i + 1], (BLOCK, 128)) for i in range(BLOCK)]
    for i in range(BLOCK):
        inv = lax.rsqrt(row_of(cols[i], i))
        coef = jnp.where(sub > i, cols[i] * inv, 0.0)
        for t in range(4):
            scaled = row_of(parts[t], i) * inv
            parts[t] = jnp.where(sub == i, scaled, parts[t] - coef * scaled)
        for j in range(i + 1, BLOCK):
            cols[j] = cols[j] - coef * (row_of(cols[j], i) * inv)
    for t in range(4):
        work[rows, 128 * t : 128 * t + 128] = parts[t]
    left = jnp.where(lane > BLOCK * panel + BLOCK - 1, parts[base // 128], 0.0)
    whole = jnp.concatenate(parts, axis=1)
    work[base : base + 128, :] = work[base : base + 128, :] - outer(left, whole)

def kernel(
    m_hbm, g_hbm, v_hbm, wt_out, lhs_out,
    m_v, g_v, v_in, bts, btr, bh, bl, vb, pt, pst, ptr, zr, pts, ph, plo,
    gx, gy, gg, wt, r1, r2, r3, wown, work, sx, sy, sz, sc, q_s,
    ss, rs, ls,
):
    f = lax.axis_index("fsdp")
    z = lax.axis_index("tensor")
    x, y, c = f // 8, lax.rem(f // 2, 4), lax.rem(f, 2)

    def mod(i):
        return lax.rem(i + 8, 4)

    def dev(xx, yy, cc, zz):
        return (mod(xx) * 8 + mod(yy) * 2 + cc, mod(zz))

    sib = dev(x, y, 1 - c, z)
    n_used = [0]

    def take(n):
        at = n_used[0]
        n_used[0] += n
        assert n_used[0] <= N_SEM
        return at

    def send(src, dst, to, i):
        return pltpu.make_async_remote_copy(
            src_ref=src, dst_ref=dst, send_sem=ss.at[i], recv_sem=rs.at[i],
            device_id=to, device_id_type=MESH,
        )

    pending = []

    def start(src, dst, to, i):
        copy = send(src, dst, to, i)
        copy.start()
        pending.append(copy)

    def arrived(dst, i):
        send(dst, dst, sib, i).wait_recv()

    def sent():
        for copy in pending:
            copy.wait_send()
        pending.clear()

    bar = pltpu.get_barrier_semaphore()
    peers = [sib]
    for d in (1, 2, 3):
        peers += [dev(x + d, y, c, z), dev(x, y + d, c, z), dev(x, y, c, z + d)]
    for peer in peers:
        pl.semaphore_signal(bar, inc=1, device_id=peer, device_id_type=MESH)
    v_load = pltpu.make_async_copy(v_hbm, v_in, ls.at[6])
    v_load.start()
    loads = []
    for h in range(2):
        half = (1 - c) if h == 0 else c
        at = pl.ds(pl.multiple_of(half * HALF, 128), HALF)
        loads.append(pltpu.make_async_copy(m_hbm.at[:, at], m_v.at[h], ls.at[2 * h]))
        loads.append(pltpu.make_async_copy(g_hbm.at[:, at], g_v.at[h], ls.at[2 * h + 1]))
    for load in loads:
        load.start()
    v_load.wait()
    pl.semaphore_wait(bar, len(peers))

    def ab(s):
        return (x, y) if s == 0 else (y, x)

    def dev_ab(s, a, b):
        return dev(a, b, c, z) if s == 0 else dev(b, a, c, z)

    class Gather:
        def __init__(self, piece, half, own):
            self.piece, self.half, self.own = piece, half, own
            self.small, self.big, self.forward = take(12), take(32), take(32)

        def i_small(self, s, u, d):
            return self.small + 6 * s + 3 * u + d - 1

        def i_big(self, s, u, way, k):
            return self.big + 16 * s + 8 * u + 4 * way + k

        def i_forward(self, s, u, way, k):
            return self.forward + 16 * s + 8 * u + 4 * way + k

        def begin(self, u):
            for s in range(2):
                a, b = ab(s)
                for d in (1, 3, 2):
                    start(self.own(s, u), self.piece(s, a, b, u), dev_ab(s, a, b + d), self.i_small(s, u, d))

        def spread(self, s, u, k, src):
            a, b = ab(s)
            here = self.piece(s, a, mod(b + k), u)
            start(src, here, dev_ab(s, a + 1, b), self.i_big(s, u, 0, k))
            start(src, here, dev_ab(s, a - 1, b), self.i_big(s, u, 1, k))

        def middle(self, u, d):
            for s in range(2):
                a, b = ab(s)
                piece = self.piece(s, a, mod(b - d), u)
                arrived(piece, self.i_small(s, u, d))
                if d == 1:
                    self.spread(s, u, 0, self.own(s, u))
                self.spread(s, u, 4 - d, piece)

        def relay(self, u, k):
            for s in range(2):
                a, b = ab(s)
                bb = mod(b + k)
                for way, step in ((0, 1), (1, -1)):
                    arrived(self.piece(s, mod(a - step), bb, u), self.i_big(s, u, way, k))
                    part = self.half(s, mod(a - step), bb, u, way)
                    start(part, part, dev_ab(s, a + step, b), self.i_forward(s, u, way, k))

        def finish(self, u, k):
            for s in range(2):
                a, b = ab(s)
                for way in range(2):
                    arrived(self.half(s, mod(a + 2), mod(b + k), u, way), self.i_forward(s, u, way, k))

    i_v = take(2)
    for s in range(2):
        theirs = pl.ds(pl.multiple_of((1 - c) * HALF + s * STREAM, 128), STREAM)
        start(v_in.at[:, theirs], vb.at[s, x, y, pl.ds(8 * c, 8)], sib, i_v + s)
    for s in range(2):
        mine = pl.ds(pl.multiple_of(c * HALF + s * STREAM, 128), STREAM)
        vb[s, x, y, pl.ds(pl.multiple_of(8 * c, 8), 8), :] = v_in[:, mine]
    for s in range(2):
        arrived(vb.at[s, x, y, pl.ds(8 * (1 - c), 8)], i_v + s)

    def v_piece(s, a, b, u):
        at = (s, a, b) if s == 0 else (s, b, a)
        return vb.at[(*at, slice(None), pl.ds(*V_SUB[u]))]

    def v_half(s, a, b, u, h):
        return v_piece(s, a, b, u).at[pl.ds(8 * h, 8)]

    gather_v = Gather(v_piece, v_half, lambda s, u: v_piece(s, *ab(s), u))
    gather_v.begin(0)
    gather_v.begin(1)

    i_b = take(N_CHUNK)
    loads[0].wait()
    loads[1].wait()

    def b_send(j):
        return send(bts.at[j], btr.at[j], sib, i_b + j)

    def other_chunk(j, carry):
        at = pl.ds(pl.multiple_of(j * CHUNK, CHUNK), CHUNK)
        bts[j] = (m_v[0, :, at] + g_v[0, :, at].astype(F32)).T
        b_send(j).start()
        return carry

    def own_chunk(j, carry):
        at = pl.ds(pl.multiple_of(j * CHUNK, CHUNK), CHUNK)
        high, low = split((m_v[1, :, at] + g_v[1, :, at].astype(F32)).T)
        bh[at, 0:ROWS] = high
        bl[at, 0:ROWS] = low
        return carry

    def sibling_chunk(j, carry):
        b_send(j).wait()
        at = pl.ds(pl.multiple_of(j * CHUNK, CHUNK), CHUNK)
        high, low = split(btr[j])
        bh[at, ROWS:] = high
        bl[at, ROWS:] = low
        return carry

    def project(a_of):
        for s in range(2):
            span = slice(s * STREAM, (s + 1) * STREAM)
            a = a_of(ab(s)[0])
            rows = (vb[s, a] if s == 0 else vb[s, :, a]).reshape(64, STREAM)
            high, low = split(rows)
            both = dot(jnp.concatenate([high, low], axis=0), bh[span, :])
            part = (both[0:64] + both[64:] + dot(high, bl[span, :])).reshape(4, 16, 2 * ROWS)
            if s == 0:
                pt[s, a] = part
            else:
                pt[s, :, a] = part

    lax.fori_loop(0, N_CHUNK, other_chunk, 0)
    for d in (1, 3, 2):
        for u in range(2):
            gather_v.middle(u, d)
    loads[2].wait()
    loads[3].wait()
    lax.fori_loop(0, N_CHUNK, own_chunk, 0)
    for u in range(2):
        gather_v.relay(u, 0)
    lax.fori_loop(0, N_CHUNK, sibling_chunk, 0)
    for k in (3, 1):
        for u in range(2):
            gather_v.relay(u, k)
    project(lambda a: a)
    for u in range(2):
        gather_v.relay(u, 2)
    project(lambda a: mod(a - 1))
    project(lambda a: mod(a + 1))
    for k in (0, 3, 1, 2):
        for u in range(2):
            gather_v.finish(u, k)

    project(lambda a: mod(a + 2))
    sent()

    i_p = take(1)
    pst[...] = (pt[0, :, :, :, ROWS:] + pt[1, :, :, :, ROWS:]).reshape(RANK, ROWS)
    start(pst, ptr, sib, i_p)
    mine = (pt[0, :, :, :, 0:ROWS] + pt[1, :, :, :, 0:ROWS]).reshape(RANK, ROWS)
    arrived(ptr, i_p)
    zr[0] = mine + ptr[...]
    near = z + 1 - 2 * lax.rem(z, 2)
    far = 3 - z
    i_z = take(4)
    tops = (pl.ds(0, 128), pl.ds(128, 128))
    for step in range(2):
        for h in range(2):
            to = near if h == step else far
            start(zr.at[2 * step, tops[h]], zr.at[2 * step + 1, tops[h]], dev(x, y, c, to), i_z + 2 * step + h)
        for h in range(2):
            arrived(zr.at[2 * step + 1, tops[h]], i_z + 2 * step + h)
            zr[2 * step + 2, tops[h], :] = zr[2 * step, tops[h], :] + zr[2 * step + 1, tops[h], :]
    p_own = zr.at[4]
    i_s = take(1)
    start(p_own, pts, sib, i_s)
    high, low = split(p_own[...].T)
    ph[0:ROWS, :] = high
    plo[0:ROWS, :] = low
    arrived(pts, i_s)
    high, low = split(pts[...].T)
    ph[ROWS:, :] = high
    plo[ROWS:, :] = low

    def exchange(slots, at, where, i):
        for d in (1, 2, 3):
            start(slots.at[at], slots.at[at], where(at + d), i + d - 1)

    def exchanged(slots, at, i):
        for d in (1, 2, 3):
            arrived(slots.at[mod(at - d)], i + d - 1)
        return slots[0] + slots[1] + slots[2] + slots[3]

    share = pl.ds(pl.multiple_of(32 * (2 * z + c), 32), 32)
    gx[x] = dot_nt(zr[4, share, :], p_own[...], HIGHEST) + dot_nt(pts[share, :], pts[...], HIGHEST)
    i_gx, i_gy, i_gz, i_gc = take(3), take(3), take(3), take(1)
    exchange(gx, x, lambda to: dev(to, y, c, z), i_gx)

    def right_part(s, a):
        row = pl.multiple_of(s * STREAM + a * 4 * PIECE, 16)
        at = pl.ds(row, 4 * PIECE)
        part = dot(bh[at, :], ph[...]) + dot(bh[at, :], plo[...]) + dot(bl[at, :], ph[...])
        wt[pl.ds(16 * s + 4 * a, 4)] = part.reshape(4, PIECE, RANK)

    i_r1, i_r2, i_r3 = take(8), take(8), take(12)

    def group(s, a):
        return pl.ds(16 * s + 4 * mod(a), 4)

    def first_sends(s):
        a, b = ab(s)
        for u in range(2):
            for way, step in ((0, 1), (1, -1)):
                part = pl.ds(*W_HALF[u][way])
                start(wt.at[group(s, a + 2), part], r1.at[s, :, part], dev_ab(s, a + step, b), i_r1 + 4 * s + 2 * u + way)

    def second_sends(u):
        sub = pl.ds(*W_SUB[u])
        for s in range(2):
            a, b = ab(s)
            for way, step in ((0, 1), (1, -1)):
                part = pl.ds(*W_HALF[u][way])
                arrived(r1.at[s, :, part], i_r1 + 4 * s + 2 * u + way)
                at = group(s, a + step)
                wt[at, part, :] = wt[at, part, :] + r1[s, :, part, :]
                start(wt.at[at, sub], r2.at[s, way, :, sub], dev_ab(s, a + step, b), i_r2 + 4 * s + 2 * u + way)

    def third_sends(u):
        sub = pl.ds(*W_SUB[u])
        for s in range(2):
            a, b = ab(s)
            for way in range(2):
                arrived(r2.at[s, way, :, sub], i_r2 + 4 * s + 2 * u + way)
            here = group(s, a)
            wt[here, sub, :] = wt[here, sub, :] + r2[s, 0, :, sub, :] + r2[s, 1, :, sub, :]
            for d in (1, 3, 2):
                start(wt.at[16 * s + 4 * a + mod(b + d), sub], r3.at[s, d - 1, sub], dev_ab(s, a, b + d), i_r3 + 6 * s + 3 * u + d - 1)

    keeps = []

    def own_sums(u):
        sub = pl.ds(*W_SUB[u])
        for s in range(2):
            a, b = ab(s)
            for d in (1, 3, 2):
                arrived(r3.at[s, d - 1, sub], i_r3 + 6 * s + 3 * u + d - 1)
            own = 16 * s + 4 * a + b
            wown[s, sub, :] = wt[own, sub, :] + r3[s, 0, sub, :] + r3[s, 1, sub, :] + r3[s, 2, sub, :]
            keep = pltpu.make_async_copy(wown.at[s, sub], wt_out.at[32 * c + own, sub], ls.at[7 + 2 * s + u])
            keep.start()
            keeps.append(keep)

    def w_piece(s, a, b, u):
        return wt_out.at[32 * c + 16 * s + 4 * a + b, pl.ds(*W_SUB[u])]

    def w_half(s, a, b, u, h):
        return wt_out.at[32 * c + 16 * s + 4 * a + b, pl.ds(*W_HALF[u][h])]

    gather_w = Gather(w_piece, w_half, lambda s, u: wown.at[s, pl.ds(*W_SUB[u])])
    i_w = take(8)

    def hand_over(n, step):
        for s in range(2):
            at = wt_out.at[pl.ds(32 * c + 16 * s + 4 * mod(ab(s)[0] + step), 4)]
            start(at, at, sib, i_w + 2 * n + s)

    def panels(low, high):
        def one(base):
            def body(p, carry):
                factor_panel(work, base, p)
                return carry

            return body

        per = 128 // BLOCK
        if low < per:
            lax.fori_loop(low, min(high, per), one(0), 0)
        if low < per <= high:
            work[128:, :] = work[128:, :] - dot_tn(work[0:128, 128:256], work[0:128, :], HIGHEST)
        if high > per:
            lax.fori_loop(max(low, per) - per, high - per, one(128), 0)

    for s in range(2):
        right_part(s, mod(ab(s)[0] + 2))
        first_sends(s)
    for s in range(2):
        right_part(s, mod(ab(s)[0] + 1))
        right_part(s, mod(ab(s)[0] - 1))
    gy[y] = exchanged(gx, x, i_gx)
    exchange(gy, y, lambda to: dev(x, to, c, z), i_gy)
    for s in range(2):
        right_part(s, ab(s)[0])
    second_sends(0)
    gg[z, c] = exchanged(gy, y, i_gy)
    for d in (1, 2, 3):
        start(gg.at[z, c], gg.at[z, c], dev(x, y, c, z + d), i_gz + d - 1)
    second_sends(1)
    for d in (1, 2, 3):
        arrived(gg.at[mod(z - d), c], i_gz + d - 1)
    start(gg.at[:, c], gg.at[:, c], sib, i_gc)
    eye = lax.broadcasted_iota(jnp.int32, (RANK, RANK), 0) == lax.broadcasted_iota(
        jnp.int32, (RANK, RANK), 1
    )
    work[:, RANK:] = eye.astype(F32)
    arrived(gg.at[:, 1 - c], i_gc)
    work[:, 0:RANK] = gg[...].reshape(RANK, RANK)

    panels(0, 1)
    third_sends(0)
    panels(1, 4)
    third_sends(1)
    panels(4, 6)
    own_sums(0)
    gather_w.begin(0)
    panels(6, 8)
    own_sums(1)
    gather_w.begin(1)

    panels(8, 10)
    for d in (1, 3, 2):
        gather_w.middle(0, d)
    panels(10, 12)
    for d in (1, 3, 2):
        gather_w.middle(1, d)
    for keep in keeps:
        keep.wait()
    hand_over(0, 0)
    panels(12, 14)
    gather_w.relay(0, 0)
    panels(14, 16)
    gather_w.relay(1, 0)

    low_inv = work.at[:, pl.ds(RANK, RANK)]
    total = jnp.zeros((1, RANK), F32)
    for s in range(2):
        right = dot_nt(wown[s], low_inv[...], HIGHEST)
        total = total + jnp.sum(right * right, axis=0, keepdims=True)
    i_qx, i_qy, i_qz, i_qc = take(3), take(3), take(3), take(1)
    sx[x] = jnp.broadcast_to(total, (8, RANK))
    exchange(sx, x, lambda to: dev(to, y, c, z), i_qx)
    gather_w.relay(0, 3)
    gather_w.relay(1, 3)
    q_s[...] = dot_nt(jnp.transpose(p_own[...]), low_inv[...], HIGHEST)
    sy[y] = exchanged(sx, x, i_qx)
    exchange(sy, y, lambda to: dev(x, to, c, z), i_qy)
    gather_w.relay(0, 1)
    gather_w.relay(1, 1)
    lhs_out[0:ROWS, :] = (-0.05 * dot(q_s[...], low_inv[...], HIGHEST)).astype(BF16)
    sz[z] = exchanged(sy, y, i_qy)
    exchange(sz, z, lambda to: dev(x, y, c, to), i_qz)
    gather_w.relay(0, 2)
    gather_w.relay(1, 2)
    hand_over(1, -1)
    hand_over(2, 1)
    sc[c] = exchanged(sz, z, i_qz)
    start(sc.at[c], sc.at[c], sib, i_qc)
    arrived(sc.at[1 - c], i_qc)
    norm = 1.0 / (jnp.sqrt((sc[0] + sc[1])[0:1, :]) + 1e-06)
    unit_scale = (M_ROWS * N_COLS / RANK) ** 0.5
    high, low = split(dot(q_s[...] * (unit_scale * norm), low_inv[...], HIGHEST))
    lhs_out[ROWS : 2 * ROWS, :] = low
    lhs_out[2 * ROWS + 16 : 3 * ROWS + 16, :] = high
    pick = lax.broadcasted_iota(jnp.int32, (16, RANK), 1) == (
        8 * f + lax.broadcasted_iota(jnp.int32, (16, RANK), 0)
    )
    high, low = split(dot(jnp.where(pick, norm, 0.0), low_inv[...], HIGHEST))
    lhs_out[2 * ROWS : 2 * ROWS + 16, :] = low
    lhs_out[3 * ROWS + 16 :, :] = high
    for k in (0, 3, 1, 2):
        for u in range(2):
            gather_w.finish(u, k)
    hand_over(3, 2)
    for n, step in enumerate((0, -1, 1, 2)):
        for s in range(2):
            at = pl.ds(32 * (1 - c) + 16 * s + 4 * mod(ab(s)[0] + step), 4)
            arrived(wt_out.at[at], i_w + 2 * n + s)
    sent()

def reduce_right(momentum, gradient, right_prev):
    vmem = pltpu.VMEM
    any_space = pl.BlockSpec(memory_space=pl.ANY)
    in_hbm = pl.BlockSpec(memory_space=pltpu.HBM)
    in_vmem = pl.BlockSpec(memory_space=pltpu.VMEM)
    return pl.pallas_call(
        kernel,
        out_shape=(
            jax.ShapeDtypeStruct((64, PIECE, RANK), F32),
            jax.ShapeDtypeStruct((3 * ROWS + 32, RANK), BF16),
        ),
        in_specs=[in_hbm, in_hbm, in_hbm],
        out_specs=(any_space, in_vmem),
        scratch_shapes=[
            vmem((2, ROWS, HALF), F32),
            vmem((2, ROWS, HALF), BF16),
            vmem((8, COLS), F32),
            vmem((N_CHUNK, CHUNK, ROWS), F32),
            vmem((N_CHUNK, CHUNK, ROWS), F32),
            vmem((HALF, 2 * ROWS), BF16),
            vmem((HALF, 2 * ROWS), BF16),
            vmem((2, 4, 4, 16, STREAM), F32),
            vmem((2, 4, 4, 16, 2 * ROWS), F32),
            vmem((RANK, ROWS), F32),
            vmem((RANK, ROWS), F32),
            vmem((5, RANK, ROWS), F32),
            vmem((RANK, ROWS), F32),
            vmem((2 * ROWS, RANK), BF16),
            vmem((2 * ROWS, RANK), BF16),
            vmem((4, 32, RANK), F32),
            vmem((4, 32, RANK), F32),
            vmem((4, 2, 32, RANK), F32),
            vmem((32, PIECE, RANK), F32),
            vmem((2, 4, PIECE, RANK), F32),
            vmem((2, 2, 4, PIECE, RANK), F32),
            vmem((2, 3, PIECE, RANK), F32),
            vmem((2, PIECE, RANK), F32),
            vmem((RANK, 2 * RANK), F32),
            vmem((4, 8, RANK), F32),
            vmem((4, 8, RANK), F32),
            vmem((4, 8, RANK), F32),
            vmem((2, 8, RANK), F32),
            vmem((ROWS, RANK), F32),
            pltpu.SemaphoreType.DMA((N_SEM,)),
            pltpu.SemaphoreType.DMA((N_SEM,)),
            pltpu.SemaphoreType.DMA((11,)),
        ],
        compiler_params=pltpu.CompilerParams(
            collective_id=0, has_side_effects=True, vmem_limit_bytes=MAIN_MIB * 2**20
        ),
        name="reduce_right",
    )(momentum, gradient, right_prev)

def finish_kernel(m, g, wt, lhs, new_hbm, right_hbm, update_hbm, new, right, update, sems):
    top = 2 * ROWS + 16
    steps = COLS // WIDE

    def copies(j, slot):
        at = pl.ds(pl.multiple_of(j * WIDE, WIDE), WIDE)
        return (
            pltpu.make_async_copy(new.at[slot], new_hbm.at[:, at], sems.at[slot]),
            pltpu.make_async_copy(update.at[slot], update_hbm.at[:, at], sems.at[2 + slot]),
        )

    def step(j, carry):
        slot = lax.rem(j, 2)
        at = pl.ds(pl.multiple_of(j * WIDE, WIDE), WIDE)
        high, low = split(wt[at, :])
        one = dot_nt(lhs[...], high)
        two = dot_nt(lhs[top:, :], low)

        @pl.when(j >= 2)
        def _():
            for copy in copies(j - 2, slot):
                copy.wait()

        new[slot] = m[:, at] + g[:, at].astype(F32) + one[0:ROWS]
        update[slot] = (one[top : top + ROWS] + (one[ROWS : 2 * ROWS] + two[0:ROWS])).astype(BF16)
        right[:, at] = (one[top + ROWS :] + (one[2 * ROWS : top] + two[ROWS:]))[0:8]
        for copy in copies(j, slot):
            copy.start()
        return carry

    lax.fori_loop(0, steps, step, 0)
    last = pltpu.make_async_copy(right, right_hbm, sems.at[4])
    last.start()
    for j in (steps - 2, steps - 1):
        for copy in copies(j, j % 2):
            copy.wait()
    last.wait()

def finish(momentum, gradient, wt, lhs):
    in_vmem = pl.BlockSpec(memory_space=pltpu.VMEM)
    any_space = pl.BlockSpec(memory_space=pl.ANY)
    return pl.pallas_call(
        finish_kernel,
        out_shape=(
            jax.ShapeDtypeStruct((ROWS, COLS), F32),
            jax.ShapeDtypeStruct((8, COLS), F32),
            jax.ShapeDtypeStruct((ROWS, COLS), BF16),
        ),
        in_specs=[in_vmem] * 4,
        out_specs=(any_space,) * 3,
        scratch_shapes=[
            pltpu.VMEM((2, ROWS, WIDE), F32),
            pltpu.VMEM((8, COLS), F32),
            pltpu.VMEM((2, ROWS, WIDE), BF16),
            pltpu.SemaphoreType.DMA((5,)),
        ],
        compiler_params=pltpu.CompilerParams(vmem_limit_bytes=FINISH_MIB * 2**20),
        name="finish",
    )(momentum, gradient, wt, lhs)

def on_device(momentum, gradient, right_prev):
    wt, lhs = reduce_right(momentum, gradient, right_prev)
    return finish(momentum, gradient, wt.reshape(COLS, RANK), lhs)

def solution(mesh):
    spec = P("fsdp", "tensor")
    return jax.shard_map(
        on_device, mesh=mesh, in_specs=(spec,) * 3, out_specs=(spec,) * 3, check_vma=False
    )
```

time: 138 us -> 113 us (0.82)
  Pallas kernels: 131 us -> 109 us
  local copies, waits for them, and re-layouts: 6.65 us -> 3.29 us
    pallas_call x1, Pallas kernels: 121 us -> 101 us  [reduce_right(): pl.pallas_call(kernel, out_shape=(jax.ShapeDtypeStruct((64, PIECE, RANK),...]
    unnamed x10 -> x6, local copies, waits for them, and re-layouts: 6.65 us -> 3.29 us
    pallas_call x1, Pallas kernels: 9.67 us -> 7.89 us  [finish(): pl.pallas_call(finish_kernel, out_shape=(jax.ShapeDtypeStruct((ROWS, COLS...]
where the time goes in v2:
time: 113 us
  Pallas kernels  109 us (96%)
  local copies, waits for them, and re-layouts  3.29 us (3%)
    pallas_call x1, Pallas kernels, reduce_right(): pl.pallas_call(kernel, out_shape=(jax.ShapeDtypeStruct((64, PIECE, RANK),...  101 us
    pallas_call x1, Pallas kernels, finish(): pl.pallas_call(finish_kernel, out_shape=(jax.ShapeDtypeStruct((ROWS, COLS...  7.89 us
    unnamed x6, local copies, waits for them, and re-layouts  3.29 us

profile of v2, /device:TPU:1, one launch (start us, length us, event | category | flops | bytes accessed | tf_op | source)
XLA Modules:
  0.0 112.9 jit_solution(6190189291194647527)
XLA Ops:
  0.6 0.0 copy-start
  0.6 0.0 copy-start.1
  0.7 2.1 %copy-done.1 = bf16[256,6656]{1,0:T(8,128)(2,1)S(1)} copy-done((bf16[256,6656]{1,0:T(8,128)(2,1)S(1)}, bf16[256,6656]{1,0:T(8,128)(2,1)}, u32[]{:S(2)}) %copy-start.1) | copy-done | bytes 3407896
  2.8 0.0 copy-start.2
  2.8 1.2 %copy-done.2 = f32[8,6656]{1,0:T(8,128)S(1)} copy-done((f32[8,6656]{1,0:T(8,128)S(1)}, f32[8,6656]{1,0:T(8,128)}, u32[]{:S(2)}) %copy-start.2) | copy-done | bytes 213016
  3.9 100.9 %reduce_right.1 = (f32[64,104,256]{2,1,0:T(8,128)S(1)}, bf16[800,256]{1,0:T(8,128)(2,1)S(1)}) custom-call(f32[256,6656]{1,0:T(8,128)} %m.1, bf16[256,6656]{1,0:T(8,128)(2,1)S(1)} %copy-done.1, f32[8,6656]{1,0:T(8,128)S(1)} %copy-done.2), custom_call_target="tpu_custom_call" | custom-call | tf_op jit(solution)/shard_map/reduce_right/pallas_call | solution.py:522
  104.8 0.0 copy-done
  104.8 7.9 %finish.1 = (f32[256,6656]{1,0:T(8,128)}, f32[8,6656]{1,0:T(8,128)}, bf16[256,6656]{1,0:T(8,128)(2,1)}) custom-call(f32[256,6656]{1,0:T(8,128)S(1)} %copy-done, bf16[256,6656]{1,0:T(8,128)(2,1)S(1)} %copy-done.1, f32[6656,256]{1,0:T(8,128)S(1)} %bitcast.1, bf16[800,256]{1,0:T(8,128)(2,1)S(1)} %get-tuple-element.6.lhs), custom_call_target="tpu_custom_call" | custom-call | tf_op jit(solution)/shard_map/finish/pallas_call | solution.py:611
Async XLA Ops:
  0.6 104.2 %copy-start = (f32[256,6656]{1,0:T(8,128)S(1)}, f32[256,6656]{1,0:T(8,128)}, u32[]{:S(2)}) copy-start(f32[256,6656]{1,0:T(8,128)} %m.1) | copy-start | bytes 20447236
  0.6 2.1 %copy-start.1 = (bf16[256,6656]{1,0:T(8,128)(2,1)S(1)}, bf16[256,6656]{1,0:T(8,128)(2,1)}, u32[]{:S(2)}) copy-start(bf16[256,6656]{1,0:T(8,128)(2,1)} %g.1) | copy-start | bytes 10223620
  2.8 1.2 %copy-start.2 = (f32[8,6656]{1,0:T(8,128)S(1)}, f32[8,6656]{1,0:T(8,128)}, u32[]{:S(2)}) copy-start(f32[8,6656]{1,0:T(8,128)} %v_hbm.1) | copy-start | bytes 638980

commit v3 on v2

--- a/solution.py
+++ b/solution.py
@@ -292,30 +292,35 @@
     project(lambda a: mod(a + 2))
     sent()
 
-    i_p = take(1)
-    pst[...] = (pt[0, :, :, :, ROWS:] + pt[1, :, :, :, ROWS:]).reshape(RANK, ROWS)
-    start(pst, ptr, sib, i_p)
-    mine = (pt[0, :, :, :, 0:ROWS] + pt[1, :, :, :, 0:ROWS]).reshape(RANK, ROWS)
-    arrived(ptr, i_p)
-    zr[0] = mine + ptr[...]
+    i_p, i_z, i_s = take(4), take(8), take(4)
+    parts = [pl.ds(64 * n, 64) for n in range(4)]
     near = z + 1 - 2 * lax.rem(z, 2)
     far = 3 - z
-    i_z = take(4)
-    tops = (pl.ds(0, 128), pl.ds(128, 128))
-    for step in range(2):
-        for h in range(2):
-            to = near if h == step else far
-            start(zr.at[2 * step, tops[h]], zr.at[2 * step + 1, tops[h]], dev(x, y, c, to), i_z + 2 * step + h)
-        for h in range(2):
-            arrived(zr.at[2 * step + 1, tops[h]], i_z + 2 * step + h)
-            zr[2 * step + 2, tops[h], :] = zr[2 * step, tops[h], :] + zr[2 * step + 1, tops[h], :]
+    for n in range(4):
+        pst[parts[n], :] = (pt[0, n, :, :, ROWS:] + pt[1, n, :, :, ROWS:]).reshape(64, ROWS)
+        start(pst.at[parts[n]], ptr.at[parts[n]], sib, i_p + n)
+    for n in range(4):
+        zr[0, parts[n], :] = (pt[0, n, :, :, 0:ROWS] + pt[1, n, :, :, 0:ROWS]).reshape(64, ROWS)
+    for step in range(3):
+        for n in range(4):
+            at = parts[n]
+            if step == 0:
+                arrived(ptr.at[at], i_p + n)
+                zr[0, at, :] = zr[0, at, :] + ptr[at, :]
+            else:
+                arrived(zr.at[2 * step - 1, at], i_z + 4 * (step - 1) + n)
+                zr[2 * step, at, :] = zr[2 * step - 2, at, :] + zr[2 * step - 1, at, :]
+            if step < 2:
+                to = near if n % 2 == step else far
+                start(zr.at[2 * step, at], zr.at[2 * step + 1, at], dev(x, y, c, to), i_z + 4 * step + n)
+            else:
+                start(zr.at[4, at], pts.at[at], sib, i_s + n)
     p_own = zr.at[4]
-    i_s = take(1)
-    start(p_own, pts, sib, i_s)
     high, low = split(p_own[...].T)
     ph[0:ROWS, :] = high
     plo[0:ROWS, :] = low
-    arrived(pts, i_s)
+    for n in range(4):
+        arrived(pts.at[parts[n]], i_s + n)
     high, low = split(pts[...].T)
     ph[ROWS:, :] = high
     plo[ROWS:, :] = low
@@ -395,7 +400,7 @@
         return wt_out.at[32 * c + 16 * s + 4 * a + b, pl.ds(*W_HALF[u][h])]
 
     gather_w = Gather(w_piece, w_half, lambda s, u: wown.at[s, pl.ds(*W_SUB[u])])
-    i_w = take(8)
+    i_w = take(14)
 
     def hand_over(n, step):
         for s in range(2):
@@ -443,30 +448,26 @@
     arrived(gg.at[:, 1 - c], i_gc)
     work[:, 0:RANK] = gg[...].reshape(RANK, RANK)
 
-    panels(0, 1)
+    panels(0, 2)
     third_sends(0)
-    panels(1, 4)
+    panels(2, 5)
     third_sends(1)
-    panels(4, 6)
+    panels(5, 8)
     own_sums(0)
     gather_w.begin(0)
-    panels(6, 8)
+    panels(8, 11)
     own_sums(1)
     gather_w.begin(1)
-
-    panels(8, 10)
+    panels(11, 13)
     for d in (1, 3, 2):
         gather_w.middle(0, d)
-    panels(10, 12)
+    panels(13, 15)
     for d in (1, 3, 2):
         gather_w.middle(1, d)
     for keep in keeps:
         keep.wait()
     hand_over(0, 0)
-    panels(12, 14)
-    gather_w.relay(0, 0)
-    panels(14, 16)
-    gather_w.relay(1, 0)
+    panels(15, 16)
 
     low_inv = work.at[:, pl.ds(RANK, RANK)]
     total = jnp.zeros((1, RANK), F32)
@@ -476,22 +477,37 @@
     i_qx, i_qy, i_qz, i_qc = take(3), take(3), take(3), take(1)
     sx[x] = jnp.broadcast_to(total, (8, RANK))
     exchange(sx, x, lambda to: dev(to, y, c, z), i_qx)
+    gather_w.relay(0, 0)
+    gather_w.relay(1, 0)
     gather_w.relay(0, 3)
     gather_w.relay(1, 3)
-    q_s[...] = dot_nt(jnp.transpose(p_own[...]), low_inv[...], HIGHEST)
     sy[y] = exchanged(sx, x, i_qx)
     exchange(sy, y, lambda to: dev(x, to, c, z), i_qy)
     gather_w.relay(0, 1)
     gather_w.relay(1, 1)
-    lhs_out[0:ROWS, :] = (-0.05 * dot(q_s[...], low_inv[...], HIGHEST)).astype(BF16)
-    sz[z] = exchanged(sy, y, i_qy)
-    exchange(sz, z, lambda to: dev(x, y, c, to), i_qz)
     gather_w.relay(0, 2)
     gather_w.relay(1, 2)
     hand_over(1, -1)
     hand_over(2, 1)
+    sz[z] = exchanged(sy, y, i_qy)
+    exchange(sz, z, lambda to: dev(x, y, c, to), i_qz)
+    q_s[...] = dot_nt(jnp.transpose(p_own[...]), low_inv[...], HIGHEST)
+    lhs_out[0:ROWS, :] = (-0.05 * dot(q_s[...], low_inv[...], HIGHEST)).astype(BF16)
+
+    def finish_piece(k):
+        for u in range(2):
+            gather_w.finish(u, k)
+        for s in range(2):
+            a, b = ab(s)
+            at = wt_out.at[32 * c + 16 * s + 4 * mod(a + 2) + mod(b + k)]
+            start(at, at, sib, i_w + 6 + 4 * s + k)
+
+    finish_piece(0)
+    finish_piece(3)
     sc[c] = exchanged(sz, z, i_qz)
     start(sc.at[c], sc.at[c], sib, i_qc)
+    finish_piece(1)
+    finish_piece(2)
     arrived(sc.at[1 - c], i_qc)
     norm = 1.0 / (jnp.sqrt((sc[0] + sc[1])[0:1, :]) + 1e-06)
     unit_scale = (M_ROWS * N_COLS / RANK) ** 0.5
@@ -504,14 +520,14 @@
     high, low = split(dot(jnp.where(pick, norm, 0.0), low_inv[...], HIGHEST))
     lhs_out[2 * ROWS : 2 * ROWS + 16, :] = low
     lhs_out[3 * ROWS + 16 :, :] = high
-    for k in (0, 3, 1, 2):
-        for u in range(2):
-            gather_w.finish(u, k)
-    hand_over(3, 2)
-    for n, step in enumerate((0, -1, 1, 2)):
-        for s in range(2):
-            at = pl.ds(32 * (1 - c) + 16 * s + 4 * mod(ab(s)[0] + step), 4)
+    for s in range(2):
+        a, b = ab(s)
+        for n, step in enumerate((0, -1, 1)):
+            at = pl.ds(32 * (1 - c) + 16 * s + 4 * mod(a + step), 4)
             arrived(wt_out.at[at], i_w + 2 * n + s)
+        for k in range(4):
+            at = 32 * (1 - c) + 16 * s + 4 * mod(a + 2) + mod(b + k)
+            arrived(wt_out.at[at], i_w + 6 + 4 * s + k)
     sent()
 
 def reduce_right(momentum, gradient, right_prev):

time: 113 us -> 109 us (0.965)
  Pallas kernels: 109 us -> 105 us
    pallas_call x1, Pallas kernels: 101 us -> 96.7 us  [reduce_right(): pl.pallas_call(kernel, out_shape=(jax.ShapeDtypeStruct((64, PIECE, RANK),...]
where the time goes in v3:
time: 109 us
  Pallas kernels  105 us (96%)
  local copies, waits for them, and re-layouts  3.29 us (3%)
    pallas_call x1, Pallas kernels, reduce_right(): pl.pallas_call(kernel, out_shape=(jax.ShapeDtypeStruct((64, PIECE, RANK),...  96.7 us
    pallas_call x1, Pallas kernels, finish(): pl.pallas_call(finish_kernel, out_shape=(jax.ShapeDtypeStruct((ROWS, COLS...  7.89 us
    unnamed x6, local copies, waits for them, and re-layouts  3.29 us

profile of v3, /device:TPU:1, one launch (start us, length us, event | category | flops | bytes accessed | tf_op | source)
XLA Modules:
  0.0 108.7 jit_solution(7018973133796917844)
XLA Ops:
  0.6 0.0 copy-start
  0.6 0.0 copy-start.1
  0.7 2.1 %copy-done.1 = bf16[256,6656]{1,0:T(8,128)(2,1)S(1)} copy-done((bf16[256,6656]{1,0:T(8,128)(2,1)S(1)}, bf16[256,6656]{1,0:T(8,128)(2,1)}, u32[]{:S(2)}) %copy-start.1) | copy-done | bytes 3407896
  2.8 0.0 copy-start.2
  2.8 1.2 %copy-done.2 = f32[8,6656]{1,0:T(8,128)S(1)} copy-done((f32[8,6656]{1,0:T(8,128)S(1)}, f32[8,6656]{1,0:T(8,128)}, u32[]{:S(2)}) %copy-start.2) | copy-done | bytes 213016
  3.9 96.7 %reduce_right.1 = (f32[64,104,256]{2,1,0:T(8,128)S(1)}, bf16[800,256]{1,0:T(8,128)(2,1)S(1)}) custom-call(f32[256,6656]{1,0:T(8,128)} %m.1, bf16[256,6656]{1,0:T(8,128)(2,1)S(1)} %copy-done.1, f32[8,6656]{1,0:T(8,128)S(1)} %copy-done.2), custom_call_target="tpu_custom_call" | custom-call | tf_op jit(solution)/shard_map/reduce_right/pallas_call | solution.py:538
  100.7 0.0 copy-done
  100.7 7.9 %finish.1 = (f32[256,6656]{1,0:T(8,128)}, f32[8,6656]{1,0:T(8,128)}, bf16[256,6656]{1,0:T(8,128)(2,1)}) custom-call(f32[256,6656]{1,0:T(8,128)S(1)} %copy-done, bf16[256,6656]{1,0:T(8,128)(2,1)S(1)} %copy-done.1, f32[6656,256]{1,0:T(8,128)S(1)} %bitcast.1, bf16[800,256]{1,0:T(8,128)(2,1)S(1)} %get-tuple-element.6.lhs), custom_call_target="tpu_custom_call" | custom-call | tf_op jit(solution)/shard_map/finish/pallas_call | solution.py:627
Async XLA Ops:
  0.6 100.0 %copy-start = (f32[256,6656]{1,0:T(8,128)S(1)}, f32[256,6656]{1,0:T(8,128)}, u32[]{:S(2)}) copy-start(f32[256,6656]{1,0:T(8,128)} %m.1) | copy-start | bytes 20447236
  0.6 2.1 %copy-start.1 = (bf16[256,6656]{1,0:T(8,128)(2,1)S(1)}, bf16[256,6656]{1,0:T(8,128)(2,1)}, u32[]{:S(2)}) copy-start(bf16[256,6656]{1,0:T(8,128)(2,1)} %g.1) | copy-start | bytes 10223620
  2.8 1.2 %copy-start.2 = (f32[8,6656]{1,0:T(8,128)S(1)}, f32[8,6656]{1,0:T(8,128)}, u32[]{:S(2)}) copy-start(f32[8,6656]{1,0:T(8,128)} %v_hbm.1) | copy-start | bytes 638980

commit v4 on v3

--- a/solution.py
+++ b/solution.py
@@ -441,6 +441,7 @@
     for d in (1, 2, 3):
         arrived(gg.at[mod(z - d), c], i_gz + d - 1)
     start(gg.at[:, c], gg.at[:, c], sib, i_gc)
+    third_sends(0)
     eye = lax.broadcasted_iota(jnp.int32, (RANK, RANK), 0) == lax.broadcasted_iota(
         jnp.int32, (RANK, RANK), 1
     )
@@ -448,35 +449,31 @@
     arrived(gg.at[:, 1 - c], i_gc)
     work[:, 0:RANK] = gg[...].reshape(RANK, RANK)
 
-    panels(0, 2)
-    third_sends(0)
-    panels(2, 5)
+    panels(0, 3)
     third_sends(1)
-    panels(5, 8)
+    panels(3, 8)
     own_sums(0)
     gather_w.begin(0)
-    panels(8, 11)
+    panels(8, 12)
     own_sums(1)
     gather_w.begin(1)
-    panels(11, 13)
     for d in (1, 3, 2):
         gather_w.middle(0, d)
-    panels(13, 15)
+    panels(12, 16)
+
+    low_inv = work.at[:, pl.ds(RANK, RANK)]
+    total = jnp.zeros((1, RANK), F32)
+    for s in range(2):
+        right = dot_nt(wown[s], low_inv[...], HIGHEST)
+        total = total + jnp.sum(right * right, axis=0, keepdims=True)
+    i_qx, i_qy, i_qz, i_qc = take(3), take(3), take(3), take(1)
+    sx[x] = jnp.broadcast_to(total, (8, RANK))
+    exchange(sx, x, lambda to: dev(to, y, c, z), i_qx)
     for d in (1, 3, 2):
         gather_w.middle(1, d)
     for keep in keeps:
         keep.wait()
     hand_over(0, 0)
-    panels(15, 16)
-
-    low_inv = work.at[:, pl.ds(RANK, RANK)]
-    total = jnp.zeros((1, RANK), F32)
-    for s in range(2):
-        right = dot_nt(wown[s], low_inv[...], HIGHEST)
-        total = total + jnp.sum(right * right, axis=0, keepdims=True)
-    i_qx, i_qy, i_qz, i_qc = take(3), take(3), take(3), take(1)
-    sx[x] = jnp.broadcast_to(total, (8, RANK))
-    exchange(sx, x, lambda to: dev(to, y, c, z), i_qx)
     gather_w.relay(0, 0)
     gather_w.relay(1, 0)
     gather_w.relay(0, 3)
@@ -588,32 +585,32 @@
     steps = COLS // WIDE
 
     def copies(j, slot):
-        at = pl.ds(pl.multiple_of(j * WIDE, WIDE), WIDE)
+        at = pl.ds(j * WIDE, WIDE)
         return (
             pltpu.make_async_copy(new.at[slot], new_hbm.at[:, at], sems.at[slot]),
             pltpu.make_async_copy(update.at[slot], update_hbm.at[:, at], sems.at[2 + slot]),
         )
 
-    def step(j, carry):
-        slot = lax.rem(j, 2)
-        at = pl.ds(pl.multiple_of(j * WIDE, WIDE), WIDE)
+    def products(j):
+        at = slice(j * WIDE, (j + 1) * WIDE)
         high, low = split(wt[at, :])
-        one = dot_nt(lhs[...], high)
-        two = dot_nt(lhs[top:, :], low)
-
-        @pl.when(j >= 2)
-        def _():
+        return dot_nt(lhs[...], high), dot_nt(lhs[top:, :], low)
+
+    ahead = products(0)
+    for j in range(steps):
+        slot = j % 2
+        at = slice(j * WIDE, (j + 1) * WIDE)
+        one, two = ahead
+        if j + 1 < steps:
+            ahead = products(j + 1)
+        if j >= 2:
             for copy in copies(j - 2, slot):
                 copy.wait()
-
         new[slot] = m[:, at] + g[:, at].astype(F32) + one[0:ROWS]
         update[slot] = (one[top : top + ROWS] + (one[ROWS : 2 * ROWS] + two[0:ROWS])).astype(BF16)
         right[:, at] = (one[top + ROWS :] + (one[2 * ROWS : top] + two[ROWS:]))[0:8]
         for copy in copies(j, slot):
             copy.start()
-        return carry
-
-    lax.fori_loop(0, steps, step, 0)
     last = pltpu.make_async_copy(right, right_hbm, sems.at[4])
     last.start()
     for j in (steps - 2, steps - 1):

time: 109 us -> 107 us (0.982)
  Pallas kernels: 105 us -> 102 us
    pallas_call x1, Pallas kernels: 96.7 us -> 95.5 us  [reduce_right(): pl.pallas_call(kernel, out_shape=(jax.ShapeDtypeStruct((64, PIECE, RANK),...]
    pallas_call x1, Pallas kernels: 7.89 us -> 6.8 us  [finish(): pl.pallas_call(finish_kernel, out_shape=(jax.ShapeDtypeStruct((ROWS, COLS...]
where the time goes in v4:
time: 107 us; the launch traced here: 106 us
  Pallas kernels  102 us (95%)
  local copies, waits for them, and re-layouts  3.29 us (3%)
    pallas_call x1, Pallas kernels, reduce_right(): pl.pallas_call(kernel, out_shape=(jax.ShapeDtypeStruct((64, PIECE, RANK),...  95.5 us
    pallas_call x1, Pallas kernels, finish(): pl.pallas_call(finish_kernel, out_shape=(jax.ShapeDtypeStruct((ROWS, COLS...  6.8 us
    unnamed x6, local copies, waits for them, and re-layouts  3.29 us

profile of v4, /device:TPU:1, one launch (start us, length us, event | category | flops | bytes accessed | tf_op | source)
XLA Modules:
  0.0 106.4 jit_solution(1723497684600094500)
XLA Ops:
  0.6 0.0 copy-start
  0.6 0.0 copy-start.1
  0.7 2.1 %copy-done.1 = bf16[256,6656]{1,0:T(8,128)(2,1)S(1)} copy-done((bf16[256,6656]{1,0:T(8,128)(2,1)S(1)}, bf16[256,6656]{1,0:T(8,128)(2,1)}, u32[]{:S(2)}) %copy-start.1) | copy-done | bytes 3407896
  2.8 0.0 copy-start.2
  2.8 1.2 %copy-done.2 = f32[8,6656]{1,0:T(8,128)S(1)} copy-done((f32[8,6656]{1,0:T(8,128)S(1)}, f32[8,6656]{1,0:T(8,128)}, u32[]{:S(2)}) %copy-start.2) | copy-done | bytes 213016
  3.9 95.5 %reduce_right.1 = (f32[64,104,256]{2,1,0:T(8,128)S(1)}, bf16[800,256]{1,0:T(8,128)(2,1)S(1)}) custom-call(f32[256,6656]{1,0:T(8,128)} %m.1, bf16[256,6656]{1,0:T(8,128)(2,1)S(1)} %copy-done.1, f32[8,6656]{1,0:T(8,128)S(1)} %copy-done.2), custom_call_target="tpu_custom_call" | custom-call | tf_op jit(solution)/shard_map/reduce_right/pallas_call | solution.py:535
  99.4 0.0 copy-done
  99.5 6.8 %finish.1 = (f32[256,6656]{1,0:T(8,128)}, f32[8,6656]{1,0:T(8,128)}, bf16[256,6656]{1,0:T(8,128)(2,1)}) custom-call(f32[256,6656]{1,0:T(8,128)S(1)} %copy-done, bf16[256,6656]{1,0:T(8,128)(2,1)S(1)} %copy-done.1, f32[6656,256]{1,0:T(8,128)S(1)} %bitcast.1, bf16[800,256]{1,0:T(8,128)(2,1)S(1)} %get-tuple-element.6.lhs), custom_call_target="tpu_custom_call" | custom-call | tf_op jit(solution)/shard_map/finish/pallas_call | solution.py:624
Async XLA Ops:
  0.6 98.8 %copy-start = (f32[256,6656]{1,0:T(8,128)S(1)}, f32[256,6656]{1,0:T(8,128)}, u32[]{:S(2)}) copy-start(f32[256,6656]{1,0:T(8,128)} %m.1) | copy-start | bytes 20447236
  0.6 2.1 %copy-start.1 = (bf16[256,6656]{1,0:T(8,128)(2,1)S(1)}, bf16[256,6656]{1,0:T(8,128)(2,1)}, u32[]{:S(2)}) copy-start(bf16[256,6656]{1,0:T(8,128)(2,1)} %g.1) | copy-start | bytes 10223620
  2.8 1.2 %copy-start.2 = (f32[8,6656]{1,0:T(8,128)S(1)}, f32[8,6656]{1,0:T(8,128)}, u32[]{:S(2)}) copy-start(f32[8,6656]{1,0:T(8,128)} %v_hbm.1) | copy-start | bytes 638980

commit v5 on v4

--- a/solution.py
+++ b/solution.py
@@ -431,9 +431,9 @@
         right_part(s, mod(ab(s)[0] - 1))
     gy[y] = exchanged(gx, x, i_gx)
     exchange(gy, y, lambda to: dev(x, to, c, z), i_gy)
+    second_sends(0)
     for s in range(2):
         right_part(s, ab(s)[0])
-    second_sends(0)
     gg[z, c] = exchanged(gy, y, i_gy)
     for d in (1, 2, 3):
         start(gg.at[z, c], gg.at[z, c], dev(x, y, c, z + d), i_gz + d - 1)

time: 107 us -> 107 us (level)
  no operation moved by 1% of the time
where the time goes in v5:
time: 107 us; the launch traced here: 106 us
  Pallas kernels  102 us (95%)
  local copies, waits for them, and re-layouts  3.29 us (3%)
    pallas_call x1, Pallas kernels, reduce_right(): pl.pallas_call(kernel, out_shape=(jax.ShapeDtypeStruct((64, PIECE, RANK),...  95.5 us
    pallas_call x1, Pallas kernels, finish(): pl.pallas_call(finish_kernel, out_shape=(jax.ShapeDtypeStruct((ROWS, COLS...  6.79 us
    unnamed x6, local copies, waits for them, and re-layouts  3.29 us

profile of v5, /device:TPU:1, one launch (start us, length us, event | category | flops | bytes accessed | tf_op | source)
XLA Modules:
  0.0 106.4 jit_solution(6718508109151132751)
XLA Ops:
  0.6 0.0 copy-start
  0.6 0.0 copy-start.1
  0.7 2.1 %copy-done.1 = bf16[256,6656]{1,0:T(8,128)(2,1)S(1)} copy-done((bf16[256,6656]{1,0:T(8,128)(2,1)S(1)}, bf16[256,6656]{1,0:T(8,128)(2,1)}, u32[]{:S(2)}) %copy-start.1) | copy-done | bytes 3407896
  2.8 0.0 copy-start.2
  2.8 1.2 %copy-done.2 = f32[8,6656]{1,0:T(8,128)S(1)} copy-done((f32[8,6656]{1,0:T(8,128)S(1)}, f32[8,6656]{1,0:T(8,128)}, u32[]{:S(2)}) %copy-start.2) | copy-done | bytes 213016
  3.9 95.5 %reduce_right.1 = (f32[64,104,256]{2,1,0:T(8,128)S(1)}, bf16[800,256]{1,0:T(8,128)(2,1)S(1)}) custom-call(f32[256,6656]{1,0:T(8,128)} %m.1, bf16[256,6656]{1,0:T(8,128)(2,1)S(1)} %copy-done.1, f32[8,6656]{1,0:T(8,128)S(1)} %copy-done.2), custom_call_target="tpu_custom_call" | custom-call | tf_op jit(solution)/shard_map/reduce_right/pallas_call | solution.py:535
  99.4 0.0 copy-done
  99.5 6.8 %finish.1 = (f32[256,6656]{1,0:T(8,128)}, f32[8,6656]{1,0:T(8,128)}, bf16[256,6656]{1,0:T(8,128)(2,1)}) custom-call(f32[256,6656]{1,0:T(8,128)S(1)} %copy-done, bf16[256,6656]{1,0:T(8,128)(2,1)S(1)} %copy-done.1, f32[6656,256]{1,0:T(8,128)S(1)} %bitcast.1, bf16[800,256]{1,0:T(8,128)(2,1)S(1)} %get-tuple-element.6.lhs), custom_call_target="tpu_custom_call" | custom-call | tf_op jit(solution)/shard_map/finish/pallas_call | solution.py:624
Async XLA Ops:
  0.6 98.8 %copy-start = (f32[256,6656]{1,0:T(8,128)S(1)}, f32[256,6656]{1,0:T(8,128)}, u32[]{:S(2)}) copy-start(f32[256,6656]{1,0:T(8,128)} %m.1) | copy-start | bytes 20447236
  0.6 2.1 %copy-start.1 = (bf16[256,6656]{1,0:T(8,128)(2,1)S(1)}, bf16[256,6656]{1,0:T(8,128)(2,1)}, u32[]{:S(2)}) copy-start(bf16[256,6656]{1,0:T(8,128)(2,1)} %g.1) | copy-start | bytes 10223620
  2.8 1.2 %copy-start.2 = (f32[8,6656]{1,0:T(8,128)S(1)}, f32[8,6656]{1,0:T(8,128)}, u32[]{:S(2)}) copy-start(f32[8,6656]{1,0:T(8,128)} %v_hbm.1) | copy-start | bytes 638980

commit v6 on v4

--- a/solution.py
+++ b/solution.py
@@ -469,6 +469,7 @@
     i_qx, i_qy, i_qz, i_qc = take(3), take(3), take(3), take(1)
     sx[x] = jnp.broadcast_to(total, (8, RANK))
     exchange(sx, x, lambda to: dev(to, y, c, z), i_qx)
+    q_s[...] = dot_nt(jnp.transpose(p_own[...]), low_inv[...], HIGHEST)
     for d in (1, 3, 2):
         gather_w.middle(1, d)
     for keep in keeps:
@@ -480,6 +481,7 @@
     gather_w.relay(1, 3)
     sy[y] = exchanged(sx, x, i_qx)
     exchange(sy, y, lambda to: dev(x, to, c, z), i_qy)
+    lhs_out[0:ROWS, :] = (-0.05 * dot(q_s[...], low_inv[...], HIGHEST)).astype(BF16)
     gather_w.relay(0, 1)
     gather_w.relay(1, 1)
     gather_w.relay(0, 2)
@@ -488,8 +490,6 @@
     hand_over(2, 1)
     sz[z] = exchanged(sy, y, i_qy)
     exchange(sz, z, lambda to: dev(x, y, c, to), i_qz)
-    q_s[...] = dot_nt(jnp.transpose(p_own[...]), low_inv[...], HIGHEST)
-    lhs_out[0:ROWS, :] = (-0.05 * dot(q_s[...], low_inv[...], HIGHEST)).astype(BF16)
 
     def finish_piece(k):
         for u in range(2):

time: 107 us -> 107 us (level)
  no operation moved by 1% of the time
where the time goes in v6:
time: 107 us; the launch traced here: 106 us
  Pallas kernels  102 us (95%)
  local copies, waits for them, and re-layouts  3.29 us (3%)
    pallas_call x1, Pallas kernels, reduce_right(): pl.pallas_call(kernel, out_shape=(jax.ShapeDtypeStruct((64, PIECE, RANK),...  95.5 us
    pallas_call x1, Pallas kernels, finish(): pl.pallas_call(finish_kernel, out_shape=(jax.ShapeDtypeStruct((ROWS, COLS...  6.79 us
    unnamed x6, local copies, waits for them, and re-layouts  3.29 us

profile of v6, /device:TPU:1, one launch (start us, length us, event | category | flops | bytes accessed | tf_op | source)
XLA Modules:
  0.0 106.4 jit_solution(11454711947057979211)
XLA Ops:
  0.6 0.0 copy-start
  0.6 0.0 copy-start.1
  0.7 2.1 %copy-done.1 = bf16[256,6656]{1,0:T(8,128)(2,1)S(1)} copy-done((bf16[256,6656]{1,0:T(8,128)(2,1)S(1)}, bf16[256,6656]{1,0:T(8,128)(2,1)}, u32[]{:S(2)}) %copy-start.1) | copy-done | bytes 3407896
  2.8 0.0 copy-start.2
  2.8 1.2 %copy-done.2 = f32[8,6656]{1,0:T(8,128)S(1)} copy-done((f32[8,6656]{1,0:T(8,128)S(1)}, f32[8,6656]{1,0:T(8,128)}, u32[]{:S(2)}) %copy-start.2) | copy-done | bytes 213016
  3.9 95.5 %reduce_right.1 = (f32[64,104,256]{2,1,0:T(8,128)S(1)}, bf16[800,256]{1,0:T(8,128)(2,1)S(1)}) custom-call(f32[256,6656]{1,0:T(8,128)} %m.1, bf16[256,6656]{1,0:T(8,128)(2,1)S(1)} %copy-done.1, f32[8,6656]{1,0:T(8,128)S(1)} %copy-done.2), custom_call_target="tpu_custom_call" | custom-call | tf_op jit(solution)/shard_map/reduce_right/pallas_call | solution.py:535
  99.4 0.0 copy-done
  99.5 6.8 %finish.1 = (f32[256,6656]{1,0:T(8,128)}, f32[8,6656]{1,0:T(8,128)}, bf16[256,6656]{1,0:T(8,128)(2,1)}) custom-call(f32[256,6656]{1,0:T(8,128)S(1)} %copy-done, bf16[256,6656]{1,0:T(8,128)(2,1)S(1)} %copy-done.1, f32[6656,256]{1,0:T(8,128)S(1)} %bitcast.1, bf16[800,256]{1,0:T(8,128)(2,1)S(1)} %get-tuple-element.6.lhs), custom_call_target="tpu_custom_call" | custom-call | tf_op jit(solution)/shard_map/finish/pallas_call | solution.py:624
Async XLA Ops:
  0.6 98.8 %copy-start = (f32[256,6656]{1,0:T(8,128)S(1)}, f32[256,6656]{1,0:T(8,128)}, u32[]{:S(2)}) copy-start(f32[256,6656]{1,0:T(8,128)} %m.1) | copy-start | bytes 20447236
  0.6 2.1 %copy-start.1 = (bf16[256,6656]{1,0:T(8,128)(2,1)S(1)}, bf16[256,6656]{1,0:T(8,128)(2,1)}, u32[]{:S(2)}) copy-start(bf16[256,6656]{1,0:T(8,128)(2,1)} %g.1) | copy-start | bytes 10223620
  2.8 1.2 %copy-start.2 = (f32[8,6656]{1,0:T(8,128)S(1)}, f32[8,6656]{1,0:T(8,128)}, u32[]{:S(2)}) copy-start(f32[8,6656]{1,0:T(8,128)} %v_hbm.1) | copy-start | bytes 638980
